TPU v7x, 512 devices: a whole 4x4x16 slice. The times are simulated.
512 devices in a mesh: page: 128 (over z, x, core), mp: 4 (over y).
Axes of the slice: x: 4, y: 4, z: 16, core: 2. Of those that a mesh axis runs over, the one named last changes fastest.
Arguments:
- queries: bfloat16 [2048, 8192], P('page', 'mp'), may hold values from -24 to 24
- cache_keys: bfloat16 [4096, 64, 1024], P('page', None, 'mp'), may hold values from -4 to 6
- cache_values: bfloat16 [4096, 64, 1024], P('page', None, 'mp'), may hold values from -6 to 6
- routes: int32 [2048, 8], P('page'), may hold values from 0 to 127, all different within a row; in each aligned block of 16 rows (0 to 15, 16 to 31, ...) at most 2 rows name the same one
- page_table: int32 [2048, 8, 2], P('page'), may hold values from 0 to 31
- lengths: int32 [2048], P('page'), may hold values from 897 to 1024
Outputs:
- attended: bfloat16 [2048, 8192], P('page', 'mp')
Inputs may be any that keep to these rules, and one draw needn't show every extreme that they name: `routes`: each request names 8 different devices; among the 16 requests of one device no device is named more than 2 times, and some device exactly 2 times.
All inputs are finite; a program needn't handle non-finite values.
Results may differ from a plain program's by a relative error of at most 0.0055.
Values may be sent and summed in bfloat16 or wider, within the bound.
No kernel may reach another device: no remote copies, remote signals or barrier semaphores. Data moves between devices by JAX's collectives and lax.ppermute only.
A program may use at most 64 MiB of HBM per device.

v0:
```python
import math

import jax
import jax.numpy as jnp
from jax import lax
from jax.sharding import PartitionSpec as P

HEAD = 128


def attend_block(query_rows, table_rows, live_count, cache_keys, cache_values, head_size):
    block_rows = query_rows.shape[0]
    pages_hop = table_rows.shape[1]
    page_len = cache_keys.shape[1]
    hop_tok = pages_hop * page_len
    kv_width = cache_keys.shape[2]
    kv_dev = kv_width // head_size
    q_dev = query_rows.shape[1] // head_size
    group = q_dev // kv_dev
    flat_pages = table_rows.reshape(-1)
    keys = cache_keys[flat_pages].reshape(block_rows, hop_tok, kv_width)
    values = cache_values[flat_pages].reshape(block_rows, hop_tok, kv_width)
    live = (jnp.arange(hop_tok, dtype=jnp.int32)[None, :] < live_count[:, None])[:, None, :]
    partial_list = []
    carry_list = []
    for kv_head in range(kv_dev):
        key_part = keys[:, :, kv_head * head_size : (kv_head + 1) * head_size]
        value_part = values[:, :, kv_head * head_size : (kv_head + 1) * head_size]
        grouped = query_rows[
            :, kv_head * group * head_size : (kv_head + 1) * group * head_size
        ].reshape(block_rows, group, head_size)
        scores = jnp.einsum(
            "sgd,std->sgt", grouped, key_part, preferred_element_type=jnp.float32
        ) * head_size ** (-0.5)
        scores = jnp.where(live, scores, jnp.float32(-1e30))
        top = jnp.max(scores, axis=-1, keepdims=True)
        probs = jnp.exp(scores - top)
        total = jnp.sum(probs, axis=-1, keepdims=True)
        weights = probs.astype(jnp.bfloat16)
        partial_value = (
            jnp.einsum("sgt,std->sgd", weights, value_part, preferred_element_type=jnp.float32)
            / total
        )
        partial_list.append(
            partial_value.astype(jnp.bfloat16).reshape(block_rows, group * head_size)
        )
        carry_list.append(top[..., 0] + jnp.log(total[..., 0]))
    return (jnp.concatenate(partial_list, axis=1), jnp.concatenate(carry_list, axis=1))


def attend(query_buf, table_buf, live_buf, cache_keys, cache_values):
    sources, count = (query_buf.shape[0], query_buf.shape[1])
    width = query_buf.shape[2]
    q_dev = width // HEAD
    rows = sources * count
    block_rows = math.gcd(rows, 32)
    blocks = rows // block_rows
    query_rows = query_buf.reshape(blocks, block_rows, width)
    table_rows = table_buf.reshape(blocks, block_rows, table_buf.shape[2])
    live_rows = live_buf.reshape(blocks, block_rows)

    def compute(items):
        return attend_block(items[0], items[1], items[2], cache_keys, cache_values, HEAD)

    def one_block(items):
        return compute(items)

    partial_value, carry = lax.map(one_block, (query_rows, table_rows, live_rows))
    return (partial_value.reshape(sources, count, width), carry.reshape(sources, count, q_dev))


def send_back(partial_value, carry):
    return (
        lax.all_to_all(partial_value, "page", split_axis=0, concat_axis=0, tiled=True),
        lax.all_to_all(carry, "page", split_axis=0, concat_axis=0, tiled=True),
    )


def per_device(queries, cache_keys, cache_values, routes, page_table, lengths):
    peers = lax.axis_size("page")
    req_dev, hops = routes.shape
    pages_hop = page_table.shape[2]
    hop_tok = pages_hop * cache_keys.shape[1]
    width = queries.shape[1]
    q_dev = width // HEAD
    slot = max(2, (2 * req_dev * hops + peers - 1) // peers)
    cells = peers * slot
    onehot = (routes[:, :, None] == jnp.arange(peers, dtype=jnp.int32)[None, None, :]).astype(
        jnp.int32
    )
    per_request = jnp.sum(onehot, axis=1)
    before = jnp.cumsum(per_request, axis=0) - per_request
    rank = jnp.take_along_axis(before, routes, axis=1)
    hop_start = jnp.arange(hops, dtype=jnp.int32)[None, :] * hop_tok
    live_hop = jnp.clip(lengths[:, None] - hop_start, 0, hop_tok)
    slot_id = (routes * slot + rank).reshape(-1)
    cell_ids = jnp.arange(cells, dtype=jnp.int32)
    placing = cell_ids[:, None] == slot_id[None, :]
    placing_req = jnp.sum(placing.reshape(cells, req_dev, hops).astype(jnp.int32), axis=2)
    query_buf = (
        jnp.dot(placing_req.astype(jnp.bfloat16), queries, preferred_element_type=jnp.float32)
        .astype(jnp.bfloat16)
        .reshape(peers, slot, width)
    )
    table_buf = jnp.dot(
        placing.astype(jnp.int32), page_table.reshape(req_dev * hops, pages_hop)
    ).reshape(peers, slot, pages_hop)
    live_buf = jnp.dot(placing.astype(jnp.int32), live_hop.reshape(-1)).reshape(peers, slot)
    partial_value, carry = attend(
        lax.all_to_all(query_buf, "page", split_axis=0, concat_axis=0, tiled=True),
        lax.all_to_all(table_buf, "page", split_axis=0, concat_axis=0, tiled=True),
        lax.all_to_all(live_buf, "page", split_axis=0, concat_axis=0, tiled=True),
        cache_keys,
        cache_values,
    )
    back_partial, back_carry = send_back(partial_value, carry)
    picking = slot_id[:, None] == cell_ids[None, :]
    pieces = jnp.dot(
        picking.astype(jnp.bfloat16),
        back_partial.reshape(cells, width),
        preferred_element_type=jnp.float32,
    ).reshape(req_dev, hops, q_dev, HEAD)
    carries = jnp.dot(
        picking.astype(jnp.float32),
        back_carry.reshape(cells, q_dev),
        precision=lax.Precision.HIGHEST,
    ).reshape(req_dev, hops, q_dev)
    high = jnp.max(carries, axis=1, keepdims=True)
    share = jnp.exp(carries - high)
    merged = jnp.sum(share[..., None] * pieces, axis=1) / jnp.sum(share, axis=1)[..., None]
    return merged.reshape(req_dev, width).astype(jnp.bfloat16)


def solution(mesh):
    placed = (
        P("page", "mp"),
        P("page", None, "mp"),
        P("page", None, "mp"),
        P("page", None),
        P("page", None, None),
        P("page"),
    )
    return jax.shard_map(
        per_device, mesh=mesh, in_specs=placed, out_specs=P("page", "mp"), check_vma=False
    )
```

profile of v0, /device:TPU:24, one launch (start us, length us, event | category | flops | bytes accessed | tf_op | source)
XLA Modules:
  0.0 278.7 jit_solution(3043023515483335565)
XLA Ops:
  1.8 1.2 gather_fusion.2
  4.7 19.8 %all-to-all-start = ((s32[128,1,2]{2,1,0:T(1,128)}), s32[128,1,2]{2,1,0:T(1,128)S(1)}, u32[]{:S(2)}, u32[]{:S(2)}) async-start(s32[128,1,2]{2,1,0:T(1,128)} %bitcast.10), calls=%async_computation | async-start | bytes 131072 | tf_op jit(solution)/shard_map/all_to_all | solution.py:112
  25.1 1.5 reshape.219
  26.6 12.3 %all-to-all-done = s32[128,1,2]{2,1,0:T(1,128)S(1)} async-done(((s32[128,1,2]{2,1,0:T(1,128)}), s32[128,1,2]{2,1,0:T(1,128)S(1)}, u32[]{:S(2)}, u32[]{:S(2)}) %all-to-all-start) | async-done | bytes 1056 | tf_op jit(solution)/shard_map/all_to_all | solution.py:112
  38.9 6.2 %all-to-all-start.1 = ((bf16[128,2,2048]{2,1,0:T(2,128)(2,1)}), bf16[128,2,2048]{2,1,0:T(2,128)(2,1)S(1)}, u32[]{:S(2)}, u32[]{:S(2)}) async-start(bf16[128,2,2048]{2,1,0:T(2,128)(2,1)} %reshape.219), calls=%async_computation.1 | async-start | bytes 2097152 | tf_op jit(solution)/shard_map/all_to_all | solution.py:110
  46.3 52.1 %all-to-all-done.1 = bf16[128,2,2048]{2,1,0:T(2,128)(2,1)S(1)} async-done(((bf16[128,2,2048]{2,1,0:T(2,128)(2,1)}), bf16[128,2,2048]{2,1,0:T(2,128)(2,1)S(1)}, u32[]{:S(2)}, u32[]{:S(2)}) %all-to-all-start.1) | async-done | bytes 1048608 | tf_op jit(solution)/shard_map/all_to_all | solution.py:110
  98.5 9.3 %all-to-all-start.2 = ((s32[128,2,2]{2,1,0:T(2,128)}), s32[128,2,2]{2,1,0:T(2,128)}, u32[]{:S(2)}, u32[]{:S(2)}) async-start(s32[128,2,2]{2,1,0:T(2,128)} %copy.52), calls=%async_computation.2 | async-start | bytes 262144 | tf_op jit(solution)/shard_map/all_to_all | solution.py:111
  109.2 1.2 reshape.220
  110.4 12.8 %all-to-all-done.2 = s32[128,2,2]{2,1,0:T(2,128)} async-done(((s32[128,2,2]{2,1,0:T(2,128)}), s32[128,2,2]{2,1,0:T(2,128)}, u32[]{:S(2)}, u32[]{:S(2)}) %all-to-all-start.2) | async-done | bytes 2080 | tf_op jit(solution)/shard_map/all_to_all | solution.py:111
  123.3 69.2 %while.12 = (s32[]{:T(128)}, bf16[8,32,2048]{2,1,0:T(8,128)(2,1)}, f32[8,32,16]{2,1,0:T(8,128)}, s32[8,32]{1,0:T(8,128)S(1)}, bf16[8,32,2048]{2,1,0:T(8,128)(2,1...) while((s32[]{:T(128)}, bf16[8,32,2048]{2,1,0:T(8,128)(2,1)}, ...), condition=%wide.region_8.9_spmd, body=%wide.region_3.0_spmd.sunk | while | flops 34411712 | bytes 15058665 | solution.py:68
  124.8 0.9 dynamic-slice_bitcast_fusion.2
  128.4 1.9 gather_fusion
  137.1 1.9 gather_fusion
  145.7 1.9 gather_fusion
  154.4 1.9 gather_fusion
  163.1 1.9 gather_fusion
  171.7 1.9 gather_fusion
  180.4 1.9 gather_fusion
  189.0 1.9 gather_fusion
  192.5 7.5 %all-to-all-start.3 = ((f32[128,2,16]{2,1,0:T(2,128)}), f32[128,2,16]{2,1,0:T(2,128)S(1)}, u32[]{:S(2)}, u32[]{:S(2)}) async-start(f32[128,2,16]{2,1,0:T(2,128)} %bitcast.12), calls=%async_computation.3 | async-start | bytes 262144 | tf_op jit(solution)/shard_map/all_to_all | solution.py:75
  200.0 2.5 reshape.225
  202.5 12.7 %all-to-all-done.3 = f32[128,2,16]{2,1,0:T(2,128)S(1)} async-done(((f32[128,2,16]{2,1,0:T(2,128)}), f32[128,2,16]{2,1,0:T(2,128)S(1)}, u32[]{:S(2)}, u32[]{:S(2)}) %all-to-all-start.3) | async-done | bytes 16416 | tf_op jit(solution)/shard_map/all_to_all | solution.py:75
  215.2 7.8 %all-to-all-start.4 = ((bf16[128,2,2048]{2,1,0:T(2,128)(2,1)}), bf16[128,2,2048]{2,1,0:T(2,128)(2,1)S(1)}, u32[]{:S(2)}, u32[]{:S(2)}) async-start(bf16[128,2,2048]{2,1,0:T(2,128)(2,1)} %reshape.225), calls=%async_computation.4 | async-start | bytes 2097152 | tf_op jit(solution)/shard_map/all_to_all | solution.py:74
  223.4 53.0 %all-to-all-done.4 = bf16[128,2,2048]{2,1,0:T(2,128)(2,1)S(1)} async-done(((bf16[128,2,2048]{2,1,0:T(2,128)(2,1)}), bf16[128,2,2048]{2,1,0:T(2,128)(2,1)S(1)}, u32[]{:S(2)}, u32[]{:S(2)}) %all-to-all-start.4) | async-done | bytes 1048608 | tf_op jit(solution)/shard_map/all_to_all | solution.py:74
  (215 shorter events, 61.5 us)
Async XLA Ops:
  0.0 24.6 %copy-start = (bf16[16,2048]{1,0:T(8,128)(2,1)S(1)}, bf16[16,2048]{1,0:T(8,128)(2,1)}, u32[]{:S(2)}) copy-start(bf16[16,2048]{1,0:T(8,128)(2,1)} %param.8) | copy-start | bytes 196612
  1.8 1.4 copy-start.2
  1.8 1.6 copy-start.4
  4.7 34.2 %all-to-all-start = ((s32[128,1,2]{2,1,0:T(1,128)}), s32[128,1,2]{2,1,0:T(1,128)S(1)}, u32[]{:S(2)}, u32[]{:S(2)}) async-start(s32[128,1,2]{2,1,0:T(1,128)} %bitcast.10), calls=%async_computation | async-start | bytes 131072 | tf_op jit(solution)/shard_map/all_to_all | solution.py:112
  25.1 20.0 %copy-start.3 = (s32[16,8,2]{0,2,1:T(2,128)S(1)}, s32[16,8,2]{0,2,1:T(2,128)}, u32[]{:S(2)}) copy-start(s32[16,8,2]{0,2,1:T(2,128)} %param.12) | copy-start | bytes 3076
  26.6 96.7 %copy-start.1 = (bf16[32,64,256]{2,1,0:T(8,128)(2,1)S(1)}, bf16[32,64,256]{2,1,0:T(8,128)(2,1)}, u32[]{:S(2)}) copy-start(bf16[32,64,256]{2,1,0:T(8,128)(2,1)} %param.9) | copy-start | bytes 3145732
  38.9 59.6 %all-to-all-start.1 = ((bf16[128,2,2048]{2,1,0:T(2,128)(2,1)}), bf16[128,2,2048]{2,1,0:T(2,128)(2,1)S(1)}, u32[]{:S(2)}, u32[]{:S(2)}) async-start(bf16[128,2,2048]{2,1,0:T(2,128)(2,1)} %reshape.219), calls=%async_computation.1 | async-start | bytes 2097152 | tf_op jit(solution)/shard_map/all_to_all | solution.py:110
  98.5 24.8 %all-to-all-start.2 = ((s32[128,2,2]{2,1,0:T(2,128)}), s32[128,2,2]{2,1,0:T(2,128)}, u32[]{:S(2)}, u32[]{:S(2)}) async-start(s32[128,2,2]{2,1,0:T(2,128)} %copy.52), calls=%async_computation.2 | async-start | bytes 262144 | tf_op jit(solution)/shard_map/all_to_all | solution.py:111
  192.5 22.7 %all-to-all-start.3 = ((f32[128,2,16]{2,1,0:T(2,128)}), f32[128,2,16]{2,1,0:T(2,128)S(1)}, u32[]{:S(2)}, u32[]{:S(2)}) async-start(f32[128,2,16]{2,1,0:T(2,128)} %bitcast.12), calls=%async_computation.3 | async-start | bytes 262144 | tf_op jit(solution)/shard_map/all_to_all | solution.py:75
  215.2 61.2 %all-to-all-start.4 = ((bf16[128,2,2048]{2,1,0:T(2,128)(2,1)}), bf16[128,2,2048]{2,1,0:T(2,128)(2,1)S(1)}, u32[]{:S(2)}, u32[]{:S(2)}) async-start(bf16[128,2,2048]{2,1,0:T(2,128)(2,1)} %reshape.225), calls=%async_computation.4 | async-start | bytes 2097152 | tf_op jit(solution)/shard_map/all_to_all | solution.py:74
where the time goes:
time: 282 us; the launch traced here: 279 us
  waiting for transfers between devices  143 us (51%)
  starting transfers between devices  50.5 us (18%)
  local copies, waits for them, and re-layouts  47.2 us (17%)
  matrix products  20.4 us (7%)
  other arithmetic  16.6 us (6%)
    all_to_all x1, waiting for transfers between devices, send_back(): lax.all_to_all(partial_value, 'page', split_axis=0, concat_axis=0, tiled=...  53 us
    all_to_all x1, waiting for transfers between devices, per_device(): lax.all_to_all(query_buf, 'page', split_axis=0, concat_axis=0, tiled=True)  52.1 us
    all_to_all x1, starting transfers between devices, per_device(): lax.all_to_all(live_buf, 'page', split_axis=0, concat_axis=0, tiled=True)  19.8 us
    gather x8, local copies, waits for them, and re-layouts, attend_block(): values = cache_values[flat_pages].reshape(block_rows, hop_tok, kv_width)  15.2 us
    all_to_all x1, waiting for transfers between devices, per_device(): lax.all_to_all(table_buf, 'page', split_axis=0, concat_axis=0, tiled=True)  12.8 us
    all_to_all x1, waiting for transfers between devices, send_back(): lax.all_to_all(carry, 'page', split_axis=0, concat_axis=0, tiled=True)  12.7 us
    all_to_all x1, waiting for transfers between devices, per_device(): lax.all_to_all(live_buf, 'page', split_axis=0, concat_axis=0, tiled=True)  12.3 us
    dot_general x16, matrix products, attend_block(): jnp.einsum('sgd,std->sgt', grouped, key_part, preferred_element_type=jnp....  11.6 us
  transfers between devices with their start and end apart: 5, of which 5 were waited for; matrix products, arithmetic and copies ran while one was open for 3% of the time, Pallas kernels for 0%

commit v1 on v0

v1 whole, which is shorter than its diff:
```python
import functools

import jax
import jax.numpy as jnp
from jax import lax
from jax.experimental import pallas as pl
from jax.experimental.pallas import tpu as pltpu
from jax.sharding import Mesh
from jax.sharding import PartitionSpec as P

HEAD = 128
HALVES = 4
SLOT = 2
DEAD = -1e30
EXTRA = 128
F32 = jnp.float32
BF16 = jnp.bfloat16


def iota(shape, dim):
    return lax.broadcasted_iota(jnp.int32, shape, dim)


def pieces(x):
    high = x.astype(BF16).astype(F32)
    mid = (x - high).astype(BF16).astype(F32)
    low = (x - high - mid).astype(BF16).astype(F32)
    return high, mid, low


def select_kernel(far, hops, base_ref, rows_ref, out_ref, sel_ref):
    count, width = rows_ref.shape
    width -= EXTRA
    cells = out_ref.shape[0]
    req_dev = count // far
    info = rows_ref[:, width:].astype(F32)
    lane = iota((count, cells), 1)
    row = iota((count, cells), 0)
    dest = (lane // (SLOT * far) + base_ref[0]).astype(F32)
    own = (lane // SLOT) % far == row // req_dev
    named = jnp.zeros((count, cells), F32)
    first = jnp.zeros((count, cells), F32)
    second = jnp.zeros((count, cells), F32)
    live = jnp.zeros((count, cells), F32)
    for hop in range(hops):
        hit = (info[:, hop : hop + 1] == dest) & own
        named = jnp.where(hit, 1.0, named)
        first = jnp.where(hit, info[:, hops + hop : hops + hop + 1], first)
        second = jnp.where(hit, info[:, 2 * hops + hop : 2 * hops + hop + 1], second)
        live = jnp.where(hit, info[:, 3 * hops + hop : 3 * hops + hop + 1], live)
    a = iota((count, count), 0)
    b = iota((count, count), 1)
    before = jnp.where((a // req_dev == b // req_dev) & (b < a), 1.0, 0.0).astype(BF16)
    rank = jnp.dot(before, named.astype(BF16), preferred_element_type=F32)
    sel = jnp.where(rank == (lane % SLOT).astype(F32), named, 0.0)
    sel_ref[...] = sel
    told = jnp.concatenate(
        [
            jnp.sum(sel * first, axis=0, keepdims=True),
            jnp.sum(sel * second, axis=0, keepdims=True),
            jnp.sum(sel * live, axis=0, keepdims=True),
            jnp.zeros((EXTRA - 3, cells), F32),
        ],
        axis=0,
    )
    out_ref[:, width:] = told.T.astype(BF16)
    place = jnp.concatenate([sel, jnp.zeros((128 - count, cells), F32)], axis=0).T.astype(BF16)
    queries = jnp.concatenate(
        [rows_ref[:, :width], jnp.zeros((128 - count, width), BF16)], axis=0
    )
    step = 256
    for col in range(0, width, step):
        out_ref[:, col : col + step] = jnp.dot(
            place, queries[:, col : col + step], preferred_element_type=F32
        ).astype(BF16)


def attend_kernel(
    rows_ref, keys_ref, values_ref, out_ref, told_ref, told_smem, q_ref, o_ref, carry_ref, sem
):
    cells, width = rows_ref.shape
    width -= EXTRA
    heads = width // HEAD
    group = heads // 2
    page_len, kv_width = keys_ref.shape[1], keys_ref.shape[2]
    hop_tok = 2 * page_len
    scale = HEAD ** -0.5
    told_ref[...] = rows_ref[:, width:].astype(F32).T[:8].astype(jnp.int32)
    copy = pltpu.make_async_copy(told_ref, told_smem, sem)
    copy.start()
    copy.wait()
    block = 16
    token = iota((heads, hop_tok), 1)
    lane = iota((heads, cells), 1)
    zero = jnp.zeros((group, HEAD), F32)

    def page(ref, which, cell):
        return ref[told_smem[which, cell]]

    def step(i, carries):
        start = pl.multiple_of(i * block, block)
        for head in range(heads):
            q_ref[head * block : (head + 1) * block, :] = rows_ref[
                pl.ds(start, block), head * HEAD : (head + 1) * HEAD
            ].astype(F32)
        for pair in range(0, block, 2):
            spread = []
            for cell in (pair, pair + 1):
                query = q_ref[pl.ds(cell, heads, stride=block), :]
                spread.append(jnp.concatenate([query[:group], zero], axis=1))
                spread.append(jnp.concatenate([zero, query[group:]], axis=1))
            spread = jnp.concatenate(spread, axis=0).astype(BF16)
            keys = jnp.concatenate(
                [page(keys_ref, which, start + cell) for cell in (pair, pair + 1) for which in (0, 1)],
                axis=0,
            )
            scores = lax.dot_general(
                spread, keys, (((1,), (1,)), ((), ())), preferred_element_type=F32
            ) * scale
            weights = []
            totals = []
            for n, cell in enumerate((pair, pair + 1)):
                own = scores[n * heads : (n + 1) * heads, n * hop_tok : (n + 1) * hop_tok]
                own = jnp.where(token < told_smem[2, start + cell], own, DEAD)
                top = jnp.max(own, axis=1, keepdims=True)
                probs = jnp.exp(own - top)
                total = jnp.sum(probs, axis=1, keepdims=True)
                carries = jnp.where(lane == start + cell, top + jnp.log(total), carries)
                nothing = jnp.zeros_like(probs)
                weights.append(
                    jnp.concatenate([probs, nothing] if n == 0 else [nothing, probs], axis=1)
                )
                totals.append(total)
            weights = jnp.concatenate(weights, axis=0).astype(BF16)
            values = jnp.concatenate(
                [page(values_ref, which, start + cell) for cell in (pair, pair + 1) for which in (0, 1)],
                axis=0,
            )
            mixed = jnp.dot(weights, values, preferred_element_type=F32)
            for n, cell in enumerate((pair, pair + 1)):
                at = n * heads
                o_ref[cell * heads : cell * heads + group, :] = (
                    mixed[at : at + group, :HEAD] / totals[n][:group]
                )
                o_ref[cell * heads + group : (cell + 1) * heads, :] = (
                    mixed[at + group : at + heads, HEAD:] / totals[n][group:]
                )
        for head in range(heads):
            out_ref[pl.ds(start, block), head * HEAD : (head + 1) * HEAD] = o_ref[
                pl.ds(head, block, stride=heads), :
            ].astype(BF16)
        return carries

    carries = lax.fori_loop(0, cells // block, step, jnp.zeros((heads, cells), F32))
    parts = pieces(carries)
    told = jnp.concatenate(
        [*parts, jnp.zeros((EXTRA - 3 * heads, cells), F32)], axis=0
    )
    out_ref[:, width:] = told.T.astype(BF16)


def merge_kernel(last, rows_ref, sel_ref, out_ref):
    cells, width = rows_ref.shape
    width -= EXTRA
    heads = width // HEAD
    count = sel_ref.shape[0]
    chosen = sel_ref[...] > 0.0
    info = rows_ref[:, width:].astype(F32)
    if cells < 128:
        info = jnp.concatenate([info, jnp.zeros((128 - cells, EXTRA), F32)], axis=0)
    info = info.T
    carries = (info[:heads] + info[heads : 2 * heads] + info[2 * heads : 3 * heads])[:, :cells]
    lane = iota((count, EXTRA), 1)
    told = jnp.zeros((count, EXTRA), F32)
    for head in range(heads):
        carry = jnp.broadcast_to(carries[head : head + 1], (count, cells))
        high = jnp.max(jnp.where(chosen, carry, DEAD), axis=1, keepdims=True)
        share = jnp.where(chosen, jnp.exp(jnp.minimum(carry - high, 0.0)), 0.0)
        total = jnp.sum(share, axis=1, keepdims=True)
        some = total > 0.0
        share = share / jnp.where(some, total, 1.0)
        major = share.astype(BF16)
        minor = (share - major.astype(F32)).astype(BF16)
        both = jnp.dot(
            jnp.concatenate([major, minor], axis=0),
            rows_ref[:, head * HEAD : (head + 1) * HEAD],
            preferred_element_type=F32,
        )
        out_ref[:, head * HEAD : (head + 1) * HEAD] = (both[:count] + both[count:]).astype(BF16)
        if not last:
            carry = jnp.where(some, high + jnp.log(jnp.where(some, total, 1.0)), DEAD)
            for n, part in enumerate(pieces(carry)):
                told = jnp.where(lane == n * heads + head, part, told)
    if not last:
        out_ref[:, width:] = told.astype(BF16)


def per_device(queries, cache_keys, cache_values, routes, page_table, lengths):
    far = lax.axis_size("far")
    near = lax.axis_size("near")
    req_dev, hops = routes.shape
    width = queries.shape[1]
    heads = width // HEAD
    hop_tok = page_table.shape[2] * cache_keys.shape[1]
    cells = near * far * SLOT
    count = far * req_dev
    full = width + EXTRA
    vmem = pl.BlockSpec(memory_space=pltpu.VMEM)
    params = pltpu.CompilerParams(vmem_limit_bytes=48 * 1024 * 1024)

    live_hop = jnp.clip(
        lengths[:, None] - jnp.arange(hops, dtype=jnp.int32)[None, :] * hop_tok, 0, hop_tok
    )
    info = jnp.concatenate([routes, page_table[:, :, 0], page_table[:, :, 1], live_hop], axis=1)
    info = jnp.pad(info, ((0, 0), (0, EXTRA - info.shape[1]))).astype(BF16)
    rows = jnp.concatenate([queries, info], axis=1)
    if far > 1:
        rows = jnp.broadcast_to(rows[None], (far, req_dev, full))
        rows = lax.all_to_all(rows, "far", split_axis=0, concat_axis=0, tiled=True)
        rows = rows.reshape(count, full)
    base = (lax.axis_index("far") * near).astype(jnp.int32).reshape(1)
    cell_rows, sel = pl.pallas_call(
        functools.partial(select_kernel, far, hops),
        out_shape=(
            jax.ShapeDtypeStruct((cells, full), BF16),
            jax.ShapeDtypeStruct((count, cells), F32),
        ),
        in_specs=[pl.BlockSpec(memory_space=pltpu.SMEM), vmem],
        out_specs=(vmem, vmem),
        compiler_params=params,
        name="select",
    )(base, rows)
    cell_rows = lax.all_to_all(
        cell_rows.reshape(near, far * SLOT, full), "near", split_axis=0, concat_axis=0, tiled=True
    ).reshape(cells, full)
    partial = pl.pallas_call(
        attend_kernel,
        out_shape=jax.ShapeDtypeStruct((cells, full), BF16),
        in_specs=[vmem] * 3,
        out_specs=vmem,
        scratch_shapes=[
            pltpu.VMEM((8, cells), jnp.int32),
            pltpu.SMEM((8, cells), jnp.int32),
            pltpu.VMEM((16 * heads, HEAD), F32),
            pltpu.VMEM((16 * heads, HEAD), F32),
            pltpu.VMEM((heads, cells), F32),
            pltpu.SemaphoreType.DMA,
        ],
        compiler_params=params,
        name="attend",
    )(cell_rows, cache_keys, cache_values)
    partial = lax.all_to_all(
        partial.reshape(near, far * SLOT, full), "near", split_axis=0, concat_axis=0, tiled=True
    ).reshape(cells, full)
    if far > 1:
        partial = pl.pallas_call(
            functools.partial(merge_kernel, False),
            out_shape=jax.ShapeDtypeStruct((count, full), BF16),
            in_specs=[vmem] * 2,
            out_specs=vmem,
            compiler_params=params,
            name="merge_near",
        )(partial, sel)
        partial = lax.all_to_all(
            partial.reshape(far, req_dev, full), "far", split_axis=0, concat_axis=0, tiled=True
        ).reshape(count, full)
        sel = (
            jnp.arange(count, dtype=jnp.int32)[None, :] % req_dev
            == jnp.arange(req_dev, dtype=jnp.int32)[:, None]
        ).astype(F32)
    return pl.pallas_call(
        functools.partial(merge_kernel, True),
        out_shape=jax.ShapeDtypeStruct((req_dev, width), BF16),
        in_specs=[vmem] * 2,
        out_specs=vmem,
        compiler_params=params,
        name="merge_far",
    )(partial, sel)


def solution(mesh):
    pages, heads = mesh.devices.shape
    fine = Mesh(mesh.devices.reshape(HALVES, pages // HALVES, heads), ("far", "near", "mp"))
    page = ("far", "near")
    placed = (
        P(page, "mp"),
        P(page, None, "mp"),
        P(page, None, "mp"),
        P(page, None),
        P(page, None, None),
        P(page),
    )
    return jax.shard_map(
        per_device, mesh=fine, in_specs=placed, out_specs=P(page, "mp"), check_vma=False
    )
```

time: 282 us -> 175 us (0.62)
  waiting for transfers between devices: 143 us -> 37.7 us
  blocking collectives: 0 us -> 71.7 us
  local copies, waits for them, and re-layouts: 47.2 us -> 0.82 us
  Pallas kernels: 0 us -> 40.9 us
  starting transfers between devices: 50.5 us -> 18.8 us
  matrix products: 20.4 us -> 0 us
  other arithmetic: 16.6 us -> 2.99 us
    all_to_all x5 -> x2, waiting for transfers between devices: 143 us -> 37.7 us  [the longest x1 18.9 us: per_device(): lax.all_to_all(partial.reshape(far, req_dev, full), 'far', split_axis=0,...]
    all_to_all x0 -> x2, blocking collectives: none -> 71.7 us  [the longest x1 38.2 us: per_device(): lax.all_to_all(cell_rows.reshape(near, far * SLOT, full), 'near', split_a...]
    pallas_call x0 -> x4, Pallas kernels: none -> 40.9 us  [the longest x1 37.3 us: per_device(): pl.pallas_call(attend_kernel, out_shape=jax.ShapeDtypeStruct((cells, full...]
    all_to_all x5 -> x2, starting transfers between devices: 50.5 us -> 18.8 us  [the longest x1 15.1 us: per_device(): rows = lax.all_to_all(rows, 'far', split_axis=0, concat_axis=0, tiled=True)]
    gather x21 -> x0, local copies, waits for them, and re-layouts: 22.2 us -> none  [the longest x8 15.2 us: attend_block(): values = cache_values[flat_pages].reshape(block_rows, hop_tok, kv_width)]
    dot_general x37 -> x0, matrix products: 20.4 us -> none  [the longest x16 11.6 us: attend_block(): jnp.einsum('sgd,std->sgt', grouped, key_part, preferred_element_type=jnp....]
    dynamic_update_slice x16 -> x0, other arithmetic: 10.7 us -> none  [attend(): lax.map(one_block, (query_rows, table_rows, live_rows))]
    squeeze x8 -> x1, local copies, waits for them, and re-layouts: 7.36 us -> 0.01 us  [per_device(): page_table[:, :, 0]]
  transfers between devices with their start and end apart: 5 -> 2, of which waited for: 5 -> 2; matrix products, arithmetic and copies ran while one was open for 3% -> 0% of each run, Pallas kernels for 0% -> 0%
where the time goes in v1:
time: 175 us; the launch traced here: 173 us
  blocking collectives  71.7 us (41%)
  Pallas kernels  40.9 us (23%)
  waiting for transfers between devices  37.7 us (22%)
  starting transfers between devices  18.8 us (11%)
  other arithmetic  2.99 us (2%)
    all_to_all x1, blocking collectives, per_device(): lax.all_to_all(cell_rows.reshape(near, far * SLOT, full), 'near', split_a...  38.2 us
    pallas_call x1, Pallas kernels, per_device(): pl.pallas_call(attend_kernel, out_shape=jax.ShapeDtypeStruct((cells, full...  37.3 us
    all_to_all x1, blocking collectives, per_device(): lax.all_to_all(partial.reshape(near, far * SLOT, full), 'near', split_axi...  33.4 us
    all_to_all x1, waiting for transfers between devices, per_device(): lax.all_to_all(partial.reshape(far, req_dev, full), 'far', split_axis=0,...  18.9 us
    all_to_all x1, waiting for transfers between devices, per_device(): rows = lax.all_to_all(rows, 'far', split_axis=0, concat_axis=0, tiled=True)  18.8 us
    all_to_all x1, starting transfers between devices, per_device(): rows = lax.all_to_all(rows, 'far', split_axis=0, concat_axis=0, tiled=True)  15.1 us
    all_to_all x1, starting transfers between devices, per_device(): lax.all_to_all(partial.reshape(far, req_dev, full), 'far', split_axis=0,...  3.69 us
  transfers between devices with their start and end apart: 2, of which 2 were waited for; matrix products, arithmetic and copies ran while one was open for 0% of the time, Pallas kernels for 0%

profile of v1, /device:TPU:24, one launch (start us, length us, event | category | flops | bytes accessed | tf_op | source)
XLA Modules:
  0.0 172.8 jit_solution(7133092855924130256)
XLA Ops:
  0.0 0.7 copy_convert_fusion
  0.7 0.7 convert.16
  1.4 0.7 clamp_convert_fusion
  2.1 0.1 copy.9
  2.2 0.9 fusion.1
  3.1 0.7 broadcast_in_dim.2
  3.8 15.1 %all-to-all-start = ((bf16[4,16,2176]{2,1,0:T(8,128)(2,1)}), bf16[4,16,2176]{2,1,0:T(8,128)(2,1)S(1)}, u32[]{:S(2)}, u32[]{:S(2)}) async-start(bf16[4,16,2176]{2,1,0:T(8,128)(2,1)} %broadcast_in_dim.2), calls=%async_computation | async-start | bytes 557056 | tf_op jit(solution)/shard_map/all_to_all | solution.py:219
  18.9 18.8 %all-to-all-done = bf16[4,16,2176]{2,1,0:T(8,128)(2,1)S(1)} async-done(((bf16[4,16,2176]{2,1,0:T(8,128)(2,1)}), bf16[4,16,2176]{2,1,0:T(8,128)(2,1)S(1)}, u32[]{:S(2)}, u32[]{:S(2)}) %all-to-all-start) | async-done | bytes 278560 | tf_op jit(solution)/shard_map/all_to_all | solution.py:219
  37.7 0.8 select.8
  38.5 0.0 copy-start
  38.5 0.0 copy-start.1
  38.5 38.2 %all_to_all.20 = bf16[32,8,2176]{2,1,0:T(8,128)(2,1)S(1)} all-to-all(bf16[32,8,2176]{2,1,0:T(8,128)(2,1)S(1)} %bitcast.15), channel_id=1, replica_groups=mesh['far'=4,'near'=32,'mp'=4] {'near'}, dimensions={0} | all-to-all | bytes 2228224 | tf_op jit(solution)/shard_map/all_to_all | solution.py:233
  76.7 0.0 copy-done
  76.7 0.0 copy-done.1
  76.7 37.3 %attend.1 = bf16[256,2176]{1,0:T(8,128)(2,1)S(1)} custom-call(bf16[256,2176]{1,0:T(8,128)(2,1)S(1)} %bitcast.13, bf16[32,64,256]{2,1,0:T(8,128)(2,1)S(1)} %copy-done, bf16[32,64,256]{2,1,0:T(8,128)(2,1)S(1)} %copy-done.1), custom_call_target="tpu_custom_call" | custom-call | tf_op jit(solution)/shard_map/attend/pallas_call | solution.py:236
  114.0 33.4 %all_to_all.21 = bf16[32,8,2176]{2,1,0:T(8,128)(2,1)S(1)} all-to-all(bf16[32,8,2176]{2,1,0:T(8,128)(2,1)S(1)} %bitcast.14), channel_id=1, replica_groups=mesh['far'=4,'near'=32,'mp'=4] {'near'}, dimensions={0} | all-to-all | bytes 2228224 | tf_op jit(solution)/shard_map/all_to_all | solution.py:252
  147.4 1.7 %merge_near.1 = bf16[64,2176]{1,0:T(8,128)(2,1)} custom-call(bf16[256,2176]{1,0:T(8,128)(2,1)S(1)} %bitcast.12, f32[64,256]{1,0:T(8,128)S(1)} %get-tuple-element.8.sel_ref), custom_call_target="tpu_custom_call" | custom-call | tf_op jit(solution)/shard_map/merge_near/pallas_call | solution.py:256
  149.2 3.7 %all-to-all-start.3 = ((bf16[4,16,2176]{2,1,0:T(8,128)(2,1)}), bf16[4,16,2176]{2,1,0:T(8,128)(2,1)S(1)}, u32[]{:S(2)}, u32[]{:S(2)}) async-start(bf16[4,16,2176]{2,1,0:T(8,128)(2,1)} %bitcast.8), calls=%async_computation.3 | async-start | bytes 557056 | tf_op jit(solution)/shard_map/all_to_all | solution.py:264
  152.9 18.9 %all-to-all-done.3 = bf16[4,16,2176]{2,1,0:T(8,128)(2,1)S(1)} async-done(((bf16[4,16,2176]{2,1,0:T(8,128)(2,1)}), bf16[4,16,2176]{2,1,0:T(8,128)(2,1)S(1)}, u32[]{:S(2)}, u32[]{:S(2)}) %all-to-all-start.3) | async-done | bytes 278560 | tf_op jit(solution)/shard_map/all_to_all | solution.py:264
  171.7 1.1 merge_far.1
  (5 shorter events, 0.0 us)
Async XLA Ops:
  3.8 33.9 %all-to-all-start = ((bf16[4,16,2176]{2,1,0:T(8,128)(2,1)}), bf16[4,16,2176]{2,1,0:T(8,128)(2,1)S(1)}, u32[]{:S(2)}, u32[]{:S(2)}) async-start(bf16[4,16,2176]{2,1,0:T(8,128)(2,1)} %broadcast_in_dim.2), calls=%async_computation | async-start | bytes 557056 | tf_op jit(solution)/shard_map/all_to_all | solution.py:219
  38.5 38.2 %copy-start = (bf16[32,64,256]{2,1,0:T(8,128)(2,1)S(1)}, bf16[32,64,256]{2,1,0:T(8,128)(2,1)}, u32[]{:S(2)}) copy-start(bf16[32,64,256]{2,1,0:T(8,128)(2,1)} %keys_ref.1) | copy-start | bytes 3145732
  38.5 38.2 %copy-start.1 = (bf16[32,64,256]{2,1,0:T(8,128)(2,1)S(1)}, bf16[32,64,256]{2,1,0:T(8,128)(2,1)}, u32[]{:S(2)}) copy-start(bf16[32,64,256]{2,1,0:T(8,128)(2,1)} %values_ref.1) | copy-start | bytes 3145732
  149.2 22.6 %all-to-all-start.3 = ((bf16[4,16,2176]{2,1,0:T(8,128)(2,1)}), bf16[4,16,2176]{2,1,0:T(8,128)(2,1)S(1)}, u32[]{:S(2)}, u32[]{:S(2)}) async-start(bf16[4,16,2176]{2,1,0:T(8,128)(2,1)} %bitcast.8), calls=%async_computation.3 | async-start | bytes 557056 | tf_op jit(solution)/shard_map/all_to_all | solution.py:264

commit v2 on v1

v2 whole, which is shorter than its diff:
```python
import functools

import jax
import jax.numpy as jnp
from jax import lax
from jax.experimental import pallas as pl
from jax.experimental.pallas import tpu as pltpu
from jax.sharding import PartitionSpec as P

HEAD = 128
FAR = 4
SLOT = 2
BLOCK = 16
DEAD = -1e30
EXTRA = 128
F32 = jnp.float32
BF16 = jnp.bfloat16


def iota(shape, dim):
    return lax.broadcasted_iota(jnp.int32, shape, dim)


def pieces(x):
    high = x.astype(BF16).astype(F32)
    mid = (x - high).astype(BF16).astype(F32)
    low = (x - high - mid).astype(BF16).astype(F32)
    return high, mid, low


def pack_kernel(hop_tok, queries_ref, routes_ref, tables_ref, lengths_ref, out_ref):
    far, req_dev, width = out_ref.shape
    width -= EXTRA
    hops = routes_ref.shape[0]
    live = jnp.clip(lengths_ref[...] - iota((hops, req_dev), 0) * hop_tok, 0, hop_tok)
    told = jnp.concatenate([routes_ref[...], live, tables_ref[...]], axis=0).astype(F32)
    told = jnp.concatenate([told, jnp.zeros((told.shape[0], 128 - req_dev), F32)], axis=1)
    told = jnp.concatenate([told, jnp.zeros((EXTRA - told.shape[0], 128), F32)], axis=0)
    told = told.T[:req_dev].astype(BF16)
    for n in range(far):
        out_ref[n, :, :width] = queries_ref[...]
        out_ref[n, :, width:] = told


def select_kernel(far, hops, base_ref, rows_ref, out_ref, sel_ref):
    count, width = rows_ref.shape
    width -= EXTRA
    cells = out_ref.shape[0]
    req_dev = count // far
    info = rows_ref[:, width:].astype(F32)
    lane = iota((count, cells), 1)
    row = iota((count, cells), 0)
    dest = (lane // (SLOT * far) + base_ref[0]).astype(F32)
    own = (lane // SLOT) % far == row // req_dev
    named = jnp.zeros((count, cells), F32)
    first = jnp.zeros((count, cells), F32)
    second = jnp.zeros((count, cells), F32)
    live = jnp.zeros((count, cells), F32)
    for hop in range(hops):
        hit = (info[:, hop : hop + 1] == dest) & own
        named = jnp.where(hit, 1.0, named)
        live = jnp.where(hit, info[:, hops + hop : hops + hop + 1], live)
        at = 2 * hops + 2 * hop
        first = jnp.where(hit, info[:, at : at + 1], first)
        second = jnp.where(hit, info[:, at + 1 : at + 2], second)
    a = iota((count, count), 0)
    b = iota((count, count), 1)
    before = jnp.where((a // req_dev == b // req_dev) & (b < a), 1.0, 0.0).astype(BF16)
    rank = jnp.dot(before, named.astype(BF16), preferred_element_type=F32)
    sel = jnp.where(rank == (lane % SLOT).astype(F32), named, 0.0)
    sel_ref[...] = sel
    told = jnp.concatenate(
        [
            jnp.sum(sel * first, axis=0, keepdims=True),
            jnp.sum(sel * second, axis=0, keepdims=True),
            jnp.sum(sel * live, axis=0, keepdims=True),
            jnp.zeros((EXTRA - 3, cells), F32),
        ],
        axis=0,
    )
    out_ref[:, width:] = told.T.astype(BF16)
    place = jnp.concatenate([sel, jnp.zeros((128 - count, cells), F32)], axis=0).T.astype(BF16)
    queries = jnp.concatenate(
        [rows_ref[:, :width], jnp.zeros((128 - count, width), BF16)], axis=0
    )
    step = 256
    for col in range(0, width, step):
        out_ref[:, col : col + step] = jnp.dot(
            place, queries[:, col : col + step], preferred_element_type=F32
        ).astype(BF16)


def attend_kernel(
    rows_ref,
    keys_ref,
    values_ref,
    out_ref,
    told_ref,
    told_smem,
    query_ref,
    score_ref,
    prob_ref,
    inverse_ref,
    mixed_ref,
    sem,
):
    cells, width = rows_ref.shape
    width -= EXTRA
    heads = width // HEAD
    group = heads // 2
    hop_tok = 2 * keys_ref.shape[1]
    scale = HEAD ** -0.5
    told_ref[...] = rows_ref[:, width:].astype(F32).T[:8].astype(jnp.int32)
    copy = pltpu.make_async_copy(told_ref, told_smem, sem)
    copy.start()
    copy.wait()
    block = BLOCK
    blocks = cells // block
    token = iota((heads, hop_tok), 1)
    lane = iota((heads, cells), 1)
    zero = jnp.zeros((group, HEAD), F32)
    nothing = jnp.zeros((heads, hop_tok), BF16)

    def pages(ref, cell):
        return jnp.concatenate(
            [ref[told_smem[which, cell + n]] for n in (0, 1) for which in (0, 1)], axis=0
        )

    def scores(i):
        start = pl.multiple_of(i * block, block)
        for head in range(heads):
            query_ref[head * block : (head + 1) * block, :] = rows_ref[
                pl.ds(start, block), head * HEAD : (head + 1) * HEAD
            ].astype(F32)
        for pair in range(0, block, 2):
            spread = []
            for cell in (pair, pair + 1):
                query = query_ref[pl.ds(cell, heads, stride=block), :]
                spread.append(jnp.concatenate([query[:group], zero], axis=1))
                spread.append(jnp.concatenate([zero, query[group:]], axis=1))
            both = lax.dot_general(
                jnp.concatenate(spread, axis=0).astype(BF16),
                pages(keys_ref, start + pair),
                (((1,), (1,)), ((), ())),
                preferred_element_type=F32,
            )
            at = pl.multiple_of((start + pair) * heads, 2 * heads)
            score_ref[pl.ds(at, heads), :] = both[:heads, :hop_tok]
            score_ref[pl.ds(at + heads, heads), :] = both[heads:, hop_tok:]

    def softmax(i, carries):
        start = pl.multiple_of(i * block, block)
        for cell in range(block):
            at = pl.multiple_of((start + cell) * heads, heads)
            own = score_ref[pl.ds(at, heads), :] * scale
            own = jnp.where(token < told_smem[2, start + cell], own, DEAD)
            top = jnp.max(own, axis=1, keepdims=True)
            probs = jnp.exp(own - top)
            total = jnp.sum(probs, axis=1, keepdims=True)
            carries = jnp.where(lane == start + cell, top + jnp.log(total), carries)
            prob_ref[pl.ds(at, heads), :] = probs.astype(BF16)
            inverse_ref[pl.ds(at, heads), :] = jnp.broadcast_to(1.0 / total, (heads, HEAD))
        return carries

    def mix(i):
        start = pl.multiple_of(i * block, block)
        for pair in range(0, block, 2):
            at = pl.multiple_of((start + pair) * heads, 2 * heads)
            one = jnp.concatenate([prob_ref[pl.ds(at, heads), :], nothing], axis=1)
            two = jnp.concatenate([nothing, prob_ref[pl.ds(at + heads, heads), :]], axis=1)
            both = jnp.dot(
                jnp.concatenate([one, two], axis=0),
                pages(values_ref, start + pair),
                preferred_element_type=F32,
            )
            inverse = inverse_ref[pl.ds(at, 2 * heads), :]
            for n in (0, 1):
                low, mid, high = n * heads, n * heads + group, (n + 1) * heads
                to = pair * heads
                mixed_ref[to + low : to + mid, :] = both[low:mid, :HEAD] * inverse[low:mid]
                mixed_ref[to + mid : to + high, :] = both[mid:high, HEAD:] * inverse[mid:high]
        for head in range(heads):
            out_ref[pl.ds(start, block), head * HEAD : (head + 1) * HEAD] = mixed_ref[
                pl.ds(head, block, stride=heads), :
            ].astype(BF16)

    def step(i, carries):
        mix(jnp.maximum(i - 2, 0))
        carries = softmax(jnp.clip(i - 1, 0, blocks - 1), carries)
        scores(jnp.minimum(i, blocks - 1))
        return carries

    carries = lax.fori_loop(0, blocks + 2, step, jnp.zeros((heads, cells), F32))
    told = jnp.concatenate(
        [*pieces(carries), jnp.zeros((EXTRA - 3 * heads, cells), F32)], axis=0
    )
    out_ref[:, width:] = told.T.astype(BF16)


def merge_kernel(last, rows_ref, sel_ref, out_ref):
    cells, width = rows_ref.shape
    width -= EXTRA
    heads = width // HEAD
    count = sel_ref.shape[0]
    chosen = sel_ref[...] > 0.0
    info = rows_ref[:, width:].astype(F32)
    if cells < 128:
        info = jnp.concatenate([info, jnp.zeros((128 - cells, EXTRA), F32)], axis=0)
    info = info.T
    carries = (info[:heads] + info[heads : 2 * heads] + info[2 * heads : 3 * heads])[:, :cells]
    lane = iota((count, EXTRA), 1)
    told = jnp.zeros((count, EXTRA), F32)
    for head in range(heads):
        carry = jnp.broadcast_to(carries[head : head + 1], (count, cells))
        high = jnp.max(jnp.where(chosen, carry, DEAD), axis=1, keepdims=True)
        share = jnp.where(chosen, jnp.exp(jnp.minimum(carry - high, 0.0)), 0.0)
        total = jnp.sum(share, axis=1, keepdims=True)
        some = total > 0.0
        share = share / jnp.where(some, total, 1.0)
        major = share.astype(BF16)
        minor = (share - major.astype(F32)).astype(BF16)
        both = jnp.dot(
            jnp.concatenate([major, minor], axis=0),
            rows_ref[:, head * HEAD : (head + 1) * HEAD],
            preferred_element_type=F32,
        )
        out_ref[:, head * HEAD : (head + 1) * HEAD] = (both[:count] + both[count:]).astype(BF16)
        if not last:
            carry = jnp.where(some, high + jnp.log(jnp.where(some, total, 1.0)), DEAD)
            for n, part in enumerate(pieces(carry)):
                told = jnp.where(lane == n * heads + head, part, told)
    if not last:
        out_ref[:, width:] = told.astype(BF16)


def far_sets(far, near):
    quarter = near // 4
    turn = [[m ^ quarter if n >= far // 2 else m for m in range(near)] for n in range(far)]
    return [[n * near + turn[n][m] for n in range(far)] for m in range(near)]


def per_device(queries, cache_keys, cache_values, routes, page_table, lengths):
    pages = lax.axis_size("page")
    far, near = FAR, pages // FAR
    near_groups = [[n * near + m for m in range(near)] for n in range(far)]
    far_groups = far_sets(far, near)
    req_dev, hops = routes.shape
    width = queries.shape[1]
    heads = width // HEAD
    hop_tok = page_table.shape[2] * cache_keys.shape[1]
    cells = near * far * SLOT
    count = far * req_dev
    full = width + EXTRA
    vmem = pl.BlockSpec(memory_space=pltpu.VMEM)
    params = pltpu.CompilerParams(vmem_limit_bytes=48 * 1024 * 1024)

    rows = pl.pallas_call(
        functools.partial(pack_kernel, hop_tok),
        out_shape=jax.ShapeDtypeStruct((far, req_dev, full), BF16),
        in_specs=[vmem] * 4,
        out_specs=vmem,
        compiler_params=params,
        name="pack",
    )(
        queries,
        routes.T,
        page_table.transpose(1, 2, 0).reshape(-1, req_dev),
        lengths.reshape(1, req_dev),
    )
    if far > 1:
        rows = lax.all_to_all(
            rows, "page", split_axis=0, concat_axis=0, axis_index_groups=far_groups, tiled=True
        )
    rows = rows.reshape(count, full)
    base = (lax.axis_index("page") // near * near).astype(jnp.int32).reshape(1)
    cell_rows, sel = pl.pallas_call(
        functools.partial(select_kernel, far, hops),
        out_shape=(
            jax.ShapeDtypeStruct((cells, full), BF16),
            jax.ShapeDtypeStruct((count, cells), F32),
        ),
        in_specs=[pl.BlockSpec(memory_space=pltpu.SMEM), vmem],
        out_specs=(vmem, vmem),
        compiler_params=params,
        name="select",
    )(base, rows)
    cell_rows = lax.all_to_all(
        cell_rows.reshape(near, far * SLOT, full), "page", split_axis=0, concat_axis=0,
        axis_index_groups=near_groups, tiled=True,
    ).reshape(cells, full)
    partial = pl.pallas_call(
        attend_kernel,
        out_shape=jax.ShapeDtypeStruct((cells, full), BF16),
        in_specs=[vmem] * 3,
        out_specs=vmem,
        scratch_shapes=[
            pltpu.VMEM((8, cells), jnp.int32),
            pltpu.SMEM((8, cells), jnp.int32),
            pltpu.VMEM((BLOCK * heads, HEAD), F32),
            pltpu.VMEM((cells * heads, HEAD), F32),
            pltpu.VMEM((cells * heads, HEAD), BF16),
            pltpu.VMEM((cells * heads, HEAD), F32),
            pltpu.VMEM((BLOCK * heads, HEAD), F32),
            pltpu.SemaphoreType.DMA,
        ],
        compiler_params=params,
        name="attend",
    )(cell_rows, cache_keys, cache_values)
    partial = lax.all_to_all(
        partial.reshape(near, far * SLOT, full), "page", split_axis=0, concat_axis=0,
        axis_index_groups=near_groups, tiled=True,
    ).reshape(cells, full)
    if far > 1:
        partial = pl.pallas_call(
            functools.partial(merge_kernel, False),
            out_shape=jax.ShapeDtypeStruct((count, full), BF16),
            in_specs=[vmem] * 2,
            out_specs=vmem,
            compiler_params=params,
            name="merge_near",
        )(partial, sel)
        partial = lax.all_to_all(
            partial.reshape(far, req_dev, full), "page", split_axis=0, concat_axis=0,
            axis_index_groups=far_groups, tiled=True,
        ).reshape(count, full)
        sel = (
            jnp.arange(count, dtype=jnp.int32)[None, :] % req_dev
            == jnp.arange(req_dev, dtype=jnp.int32)[:, None]
        ).astype(F32)
    return pl.pallas_call(
        functools.partial(merge_kernel, True),
        out_shape=jax.ShapeDtypeStruct((req_dev, width), BF16),
        in_specs=[vmem] * 2,
        out_specs=vmem,
        compiler_params=params,
        name="merge_far",
    )(partial, sel)


def solution(mesh):
    placed = (
        P("page", "mp"),
        P("page", None, "mp"),
        P("page", None, "mp"),
        P("page", None),
        P("page", None, None),
        P("page"),
    )
    return jax.shard_map(
        per_device, mesh=mesh, in_specs=placed, out_specs=P("page", "mp"), check_vma=False
    )
```

time: 175 us -> 151 us (0.86)
  Pallas kernels: 40.9 us -> 16.2 us
  other arithmetic: 2.99 us -> 0.01 us
  blocking collectives: 71.7 us -> 74.3 us
  local copies, waits for them, and re-layouts: 0.82 us -> 2.89 us
    pallas_call x1, Pallas kernels: 37.3 us -> 11.7 us  [per_device(): pl.pallas_call(attend_kernel, out_shape=jax.ShapeDtypeStruct((cells, full...]
    unnamed x5 -> x12, local copies, waits for them, and re-layouts: 0.09 us -> 2.89 us
    all_to_all x2, blocking collectives: 71.7 us -> 74.3 us  [the longest x1 40.9 us: per_device(): lax.all_to_all(cell_rows.reshape(near, far * SLOT, full), 'page', split_a...]
    another operation x3 -> x0, other arithmetic: 2.12 us -> none
where the time goes in v2:
time: 151 us; the launch traced here: 149 us
  blocking collectives  74.3 us (49%)
  waiting for transfers between devices  37.6 us (25%)
  starting transfers between devices  18.1 us (12%)
  Pallas kernels  16.2 us (11%)
  local copies, waits for them, and re-layouts  2.89 us (2%)
    all_to_all x1, blocking collectives, per_device(): lax.all_to_all(cell_rows.reshape(near, far * SLOT, full), 'page', split_a...  40.9 us
    all_to_all x1, blocking collectives, per_device(): lax.all_to_all(partial.reshape(near, far * SLOT, full), 'page', split_axi...  33.4 us
    all_to_all x1, waiting for transfers between devices, per_device(): lax.all_to_all(partial.reshape(far, req_dev, full), 'page', split_axis=0,...  20.7 us
    all_to_all x1, waiting for transfers between devices, per_device(): lax.all_to_all(rows, 'page', split_axis=0, concat_axis=0, axis_index_grou...  16.9 us
    all_to_all x1, starting transfers between devices, per_device(): lax.all_to_all(rows, 'page', split_axis=0, concat_axis=0, axis_index_grou...  14.6 us
    pallas_call x1, Pallas kernels, per_device(): pl.pallas_call(attend_kernel, out_shape=jax.ShapeDtypeStruct((cells, full...  11.7 us
    all_to_all x1, starting transfers between devices, per_device(): lax.all_to_all(partial.reshape(far, req_dev, full), 'page', split_axis=0,...  3.45 us
  transfers between devices with their start and end apart: 2, of which 2 were waited for; matrix products, arithmetic and copies ran while one was open for 0% of the time, Pallas kernels for 0%

profile of v2, /device:TPU:24, one launch (start us, length us, event | category | flops | bytes accessed | tf_op | source)
XLA Modules:
  0.0 149.1 jit_solution(9784374164069391651)
XLA Ops:
  0.0 0.0 copy-start.2
  0.0 0.8 copy-done.2
  0.8 0.0 copy-start.3
  0.8 0.7 copy-done.3
  1.5 0.0 copy-start.4
  1.5 0.7 copy-done.4
  2.2 0.0 copy-start.5
  2.2 0.7 copy-done.5
  2.9 0.8 pack.1
  3.7 14.6 %all-to-all-start = ((bf16[4,16,2176]{2,1,0:T(8,128)(2,1)}), bf16[4,16,2176]{2,1,0:T(8,128)(2,1)S(1)}, u32[]{:S(2)}, u32[]{:S(2)}) async-start(bf16[4,16,2176]{2,1,0:T(8,128)(2,1)} %pack.1), calls=%async_computation | async-start | bytes 557056 | tf_op jit(solution)/shard_map/all_to_all | solution.py:271
  18.3 16.9 %all-to-all-done = bf16[4,16,2176]{2,1,0:T(8,128)(2,1)S(1)} async-done(((bf16[4,16,2176]{2,1,0:T(8,128)(2,1)}), bf16[4,16,2176]{2,1,0:T(8,128)(2,1)S(1)}, u32[]{:S(2)}, u32[]{:S(2)}) %all-to-all-start) | async-done | bytes 278560 | tf_op jit(solution)/shard_map/all_to_all | solution.py:271
  35.2 0.8 select.7
  36.0 0.0 copy-start
  36.0 0.0 copy-start.1
  36.0 40.9 %all_to_all.20 = bf16[32,8,2176]{2,1,0:T(8,128)(2,1)S(1)} all-to-all(bf16[32,8,2176]{2,1,0:T(8,128)(2,1)S(1)} %bitcast.16), channel_id=1, replica_groups={{0,4,8,12,16,20,24,28,32,36,40,44,48,52,56,60,64,68,72,76,80,84,88,92,9..., dimensions={0} | all-to-all | bytes 2228224 | tf_op jit(solution)/shard_map/all_to_all | solution.py:287
  76.9 0.0 copy-done
  76.9 0.0 copy-done.1
  76.9 11.7 %attend.1 = bf16[256,2176]{1,0:T(8,128)(2,1)S(1)} custom-call(bf16[256,2176]{1,0:T(8,128)(2,1)S(1)} %bitcast.14, bf16[32,64,256]{2,1,0:T(8,128)(2,1)S(1)} %copy-done, bf16[32,64,256]{2,1,0:T(8,128)(2,1)S(1)} %copy-done.1), custom_call_target="tpu_custom_call" | custom-call | tf_op jit(solution)/shard_map/attend/pallas_call | solution.py:291
  88.6 33.4 %all_to_all.21 = bf16[32,8,2176]{2,1,0:T(8,128)(2,1)S(1)} all-to-all(bf16[32,8,2176]{2,1,0:T(8,128)(2,1)S(1)} %bitcast.15), channel_id=1, replica_groups={{0,4,8,12,16,20,24,28,32,36,40,44,48,52,56,60,64,68,72,76,80,84,88,92,9..., dimensions={0} | all-to-all | bytes 2228224 | tf_op jit(solution)/shard_map/all_to_all | solution.py:309
  122.1 1.7 %merge_near.1 = bf16[64,2176]{1,0:T(8,128)(2,1)} custom-call(bf16[256,2176]{1,0:T(8,128)(2,1)S(1)} %bitcast.13, f32[64,256]{1,0:T(8,128)S(1)} %get-tuple-element.8.sel_ref), custom_call_target="tpu_custom_call" | custom-call | tf_op jit(solution)/shard_map/merge_near/pallas_call | solution.py:314
  123.8 3.4 %all-to-all-start.3 = ((bf16[4,16,2176]{2,1,0:T(8,128)(2,1)}), bf16[4,16,2176]{2,1,0:T(8,128)(2,1)S(1)}, u32[]{:S(2)}, u32[]{:S(2)}) async-start(bf16[4,16,2176]{2,1,0:T(8,128)(2,1)} %bitcast.10), calls=%async_computation.3 | async-start | bytes 557056 | tf_op jit(solution)/shard_map/all_to_all | solution.py:322
  127.3 20.7 %all-to-all-done.3 = bf16[4,16,2176]{2,1,0:T(8,128)(2,1)S(1)} async-done(((bf16[4,16,2176]{2,1,0:T(8,128)(2,1)}), bf16[4,16,2176]{2,1,0:T(8,128)(2,1)S(1)}, u32[]{:S(2)}, u32[]{:S(2)}) %all-to-all-start.3) | async-done | bytes 278560 | tf_op jit(solution)/shard_map/all_to_all | solution.py:322
  148.0 1.1 merge_far.1
  (2 shorter events, 0.0 us)
Async XLA Ops:
  0.0 0.8 copy-start.2
  0.8 0.7 copy-start.3
  1.5 0.7 copy-start.4
  2.2 0.7 copy-start.5
  3.7 31.5 %all-to-all-start = ((bf16[4,16,2176]{2,1,0:T(8,128)(2,1)}), bf16[4,16,2176]{2,1,0:T(8,128)(2,1)S(1)}, u32[]{:S(2)}, u32[]{:S(2)}) async-start(bf16[4,16,2176]{2,1,0:T(8,128)(2,1)} %pack.1), calls=%async_computation | async-start | bytes 557056 | tf_op jit(solution)/shard_map/all_to_all | solution.py:271
  36.0 40.9 %copy-start = (bf16[32,64,256]{2,1,0:T(8,128)(2,1)S(1)}, bf16[32,64,256]{2,1,0:T(8,128)(2,1)}, u32[]{:S(2)}) copy-start(bf16[32,64,256]{2,1,0:T(8,128)(2,1)} %keys_ref.1) | copy-start | bytes 3145732
  36.0 40.9 %copy-start.1 = (bf16[32,64,256]{2,1,0:T(8,128)(2,1)S(1)}, bf16[32,64,256]{2,1,0:T(8,128)(2,1)}, u32[]{:S(2)}) copy-start(bf16[32,64,256]{2,1,0:T(8,128)(2,1)} %values_ref.1) | copy-start | bytes 3145732
  123.8 24.2 %all-to-all-start.3 = ((bf16[4,16,2176]{2,1,0:T(8,128)(2,1)}), bf16[4,16,2176]{2,1,0:T(8,128)(2,1)S(1)}, u32[]{:S(2)}, u32[]{:S(2)}) async-start(bf16[4,16,2176]{2,1,0:T(8,128)(2,1)} %bitcast.10), calls=%async_computation.3 | async-start | bytes 557056 | tf_op jit(solution)/shard_map/all_to_all | solution.py:322

commit v3 on v2

--- a/solution.py
+++ b/solution.py
@@ -8,7 +8,8 @@
 from jax.sharding import PartitionSpec as P
 
 HEAD = 128
-FAR = 4
+FAR = 8
+PLANE = 8
 SLOT = 2
 BLOCK = 16
 DEAD = -1e30
@@ -28,9 +29,27 @@
     return high, mid, low
 
 
-def pack_kernel(hop_tok, queries_ref, routes_ref, tables_ref, lengths_ref, out_ref):
+def pack_kernel(
+    hop_tok, queries_in, routes_in, tables_in, lengths_in, out_ref,
+    queries_ref, routes_ref, tables_ref, lengths_ref, sems,
+):
     far, req_dev, width = out_ref.shape
     width -= EXTRA
+    copies = [
+        pltpu.make_async_copy(a, b, sems.at[n])
+        for n, (a, b) in enumerate(
+            [
+                (queries_in, queries_ref),
+                (routes_in, routes_ref),
+                (tables_in, tables_ref),
+                (lengths_in, lengths_ref),
+            ]
+        )
+    ]
+    for copy in copies:
+        copy.start()
+    for copy in copies:
+        copy.wait()
     hops = routes_ref.shape[0]
     live = jnp.clip(lengths_ref[...] - iota((hops, req_dev), 0) * hop_tok, 0, hop_tok)
     told = jnp.concatenate([routes_ref[...], live, tables_ref[...]], axis=0).astype(F32)
@@ -79,14 +98,11 @@
         axis=0,
     )
     out_ref[:, width:] = told.T.astype(BF16)
-    place = jnp.concatenate([sel, jnp.zeros((128 - count, cells), F32)], axis=0).T.astype(BF16)
-    queries = jnp.concatenate(
-        [rows_ref[:, :width], jnp.zeros((128 - count, width), BF16)], axis=0
-    )
+    place = sel.T.astype(BF16)
     step = 256
     for col in range(0, width, step):
         out_ref[:, col : col + step] = jnp.dot(
-            place, queries[:, col : col + step], preferred_element_type=F32
+            place, rows_ref[:, col : col + step], preferred_element_type=F32
         ).astype(BF16)
 
 
@@ -234,8 +250,7 @@
 
 
 def far_sets(far, near):
-    quarter = near // 4
-    turn = [[m ^ quarter if n >= far // 2 else m for m in range(near)] for n in range(far)]
+    turn = [[m ^ PLANE if n >= far // 2 else m for m in range(near)] for n in range(far)]
     return [[n * near + turn[n][m] for n in range(far)] for m in range(near)]
 
 
@@ -257,9 +272,16 @@
     rows = pl.pallas_call(
         functools.partial(pack_kernel, hop_tok),
         out_shape=jax.ShapeDtypeStruct((far, req_dev, full), BF16),
-        in_specs=[vmem] * 4,
+        in_specs=[pl.BlockSpec(memory_space=pl.ANY)] * 4,
         out_specs=vmem,
-        compiler_params=params,
+        scratch_shapes=[
+            pltpu.VMEM((req_dev, width), BF16),
+            pltpu.VMEM((hops, req_dev), jnp.int32),
+            pltpu.VMEM((hops * page_table.shape[2], req_dev), jnp.int32),
+            pltpu.VMEM((1, req_dev), jnp.int32),
+            pltpu.SemaphoreType.DMA((4,)),
+        ],
+        compiler_params=pltpu.CompilerParams(vmem_limit_bytes=60 * 1024 * 1024),
         name="pack",
     )(
         queries,

time: 151 us -> 144 us (0.954); the launches traced: 149 us -> 144 us
  blocking collectives: 74.3 us -> 41.3 us
  waiting for transfers between devices: 37.6 us -> 65.2 us
  local copies, waits for them, and re-layouts: 2.89 us -> 0.01 us
  Pallas kernels: 16.2 us -> 18.5 us
    all_to_all x1, blocking collectives: 40.9 us -> 21.5 us  [per_device(): lax.all_to_all(cell_rows.reshape(near, far * SLOT, full), 'page', split_a...]
    all_to_all x1, waiting for transfers between devices: 16.9 us -> 32.5 us  [per_device(): lax.all_to_all(rows, 'page', split_axis=0, concat_axis=0, axis_index_grou...]
    all_to_all x1, blocking collectives: 33.4 us -> 19.8 us  [per_device(): lax.all_to_all(partial.reshape(near, far * SLOT, full), 'page', split_axi...]
    all_to_all x1, waiting for transfers between devices: 20.7 us -> 32.7 us  [per_device(): lax.all_to_all(partial.reshape(far, req_dev, full), 'page', split_axis=0,...]
    unnamed x12 -> x4, local copies, waits for them, and re-layouts: 2.89 us -> 0.01 us
where the time goes in v3:
time: 144 us
  waiting for transfers between devices  65.2 us (45%)
  blocking collectives  41.3 us (29%)
  starting transfers between devices  18.9 us (13%)
  Pallas kernels  18.5 us (13%)
    all_to_all x1, waiting for transfers between devices, per_device(): lax.all_to_all(partial.reshape(far, req_dev, full), 'page', split_axis=0,...  32.7 us
    all_to_all x1, waiting for transfers between devices, per_device(): lax.all_to_all(rows, 'page', split_axis=0, concat_axis=0, axis_index_grou...  32.5 us
    all_to_all x1, blocking collectives, per_device(): lax.all_to_all(cell_rows.reshape(near, far * SLOT, full), 'page', split_a...  21.5 us
    all_to_all x1, blocking collectives, per_device(): lax.all_to_all(partial.reshape(near, far * SLOT, full), 'page', split_axi...  19.8 us
    all_to_all x1, starting transfers between devices, per_device(): lax.all_to_all(rows, 'page', split_axis=0, concat_axis=0, axis_index_grou...  14.7 us
    pallas_call x1, Pallas kernels, per_device(): pl.pallas_call(attend_kernel, out_shape=jax.ShapeDtypeStruct((cells, full...  11.7 us
    all_to_all x1, starting transfers between devices, per_device(): lax.all_to_all(partial.reshape(far, req_dev, full), 'page', split_axis=0,...  4.23 us
  transfers between devices with their start and end apart: 2, of which 2 were waited for; matrix products, arithmetic and copies ran while one was open for 0% of the time, Pallas kernels for 0%

profile of v3, /device:TPU:24, one launch (start us, length us, event | category | flops | bytes accessed | tf_op | source)
XLA Modules:
  0.0 144.0 jit_solution(10104214227729137697)
XLA Ops:
  0.0 1.8 %pack.1 = bf16[8,16,2176]{2,1,0:T(8,128)(2,1)} custom-call(bf16[16,2048]{1,0:T(8,128)(2,1)} %queries_in.1, s32[8,16]{1,0:T(8,128)} %bitcast.20, s32[16,16]{1,0:T(8,128)} %bitcast.19, s32[1,16]{1,0:T(1,128)} %bitcast.21), custom_call_target="tpu_custom_call" | custom-call | tf_op jit(solution)/shard_map/pack/pallas_call | solution.py:272
  1.8 14.7 %all-to-all-start = ((bf16[8,16,2176]{2,1,0:T(8,128)(2,1)}), bf16[8,16,2176]{2,1,0:T(8,128)(2,1)S(1)}, u32[]{:S(2)}, u32[]{:S(2)}) async-start(bf16[8,16,2176]{2,1,0:T(8,128)(2,1)} %pack.1), calls=%async_computation | async-start | bytes 1114112 | tf_op jit(solution)/shard_map/all_to_all | solution.py:293
  16.4 32.5 %all-to-all-done = bf16[8,16,2176]{2,1,0:T(8,128)(2,1)S(1)} async-done(((bf16[8,16,2176]{2,1,0:T(8,128)(2,1)}), bf16[8,16,2176]{2,1,0:T(8,128)(2,1)S(1)}, u32[]{:S(2)}, u32[]{:S(2)}) %all-to-all-start) | async-done | bytes 557088 | tf_op jit(solution)/shard_map/all_to_all | solution.py:293
  49.0 1.1 select.7
  50.1 0.0 copy-start
  50.1 0.0 copy-start.1
  50.1 21.5 %all_to_all.20 = bf16[16,16,2176]{2,1,0:T(8,128)(2,1)S(1)} all-to-all(bf16[16,16,2176]{2,1,0:T(8,128)(2,1)S(1)} %bitcast.18), channel_id=1, replica_groups={{0,4,8,12,16,20,24,28,32,36,40,44,48,52,56,60},{64,68,72,76,80,84,88,92..., dimensions={0} | all-to-all | bytes 2228224 | tf_op jit(solution)/shard_map/all_to_all | solution.py:309
  71.6 0.0 copy-done
  71.6 0.0 copy-done.1
  71.6 11.7 %attend.1 = bf16[256,2176]{1,0:T(8,128)(2,1)S(1)} custom-call(bf16[256,2176]{1,0:T(8,128)(2,1)S(1)} %bitcast.14, bf16[32,64,256]{2,1,0:T(8,128)(2,1)S(1)} %copy-done, bf16[32,64,256]{2,1,0:T(8,128)(2,1)S(1)} %copy-done.1), custom_call_target="tpu_custom_call" | custom-call | tf_op jit(solution)/shard_map/attend/pallas_call | solution.py:313
  83.4 19.8 %all_to_all.21 = bf16[16,16,2176]{2,1,0:T(8,128)(2,1)S(1)} all-to-all(bf16[16,16,2176]{2,1,0:T(8,128)(2,1)S(1)} %bitcast.15), channel_id=1, replica_groups={{0,4,8,12,16,20,24,28,32,36,40,44,48,52,56,60},{64,68,72,76,80,84,88,92..., dimensions={0} | all-to-all | bytes 2228224 | tf_op jit(solution)/shard_map/all_to_all | solution.py:331
  103.2 2.7 %merge_near.1 = bf16[128,2176]{1,0:T(8,128)(2,1)} custom-call(bf16[256,2176]{1,0:T(8,128)(2,1)S(1)} %bitcast.13, f32[128,256]{1,0:T(8,128)S(1)} %get-tuple-element.8.sel_ref), custom_call_target="tpu_custom_call" | custom-call | tf_op jit(solution)/shard_map/merge_near/pallas_call | solution.py:336
  105.9 4.2 %all-to-all-start.3 = ((bf16[8,16,2176]{2,1,0:T(8,128)(2,1)}), bf16[8,16,2176]{2,1,0:T(8,128)(2,1)S(1)}, u32[]{:S(2)}, u32[]{:S(2)}) async-start(bf16[8,16,2176]{2,1,0:T(8,128)(2,1)} %bitcast.10), calls=%async_computation.3 | async-start | bytes 1114112 | tf_op jit(solution)/shard_map/all_to_all | solution.py:344
  110.1 32.7 %all-to-all-done.3 = bf16[8,16,2176]{2,1,0:T(8,128)(2,1)S(1)} async-done(((bf16[8,16,2176]{2,1,0:T(8,128)(2,1)}), bf16[8,16,2176]{2,1,0:T(8,128)(2,1)S(1)}, u32[]{:S(2)}, u32[]{:S(2)}) %all-to-all-start.3) | async-done | bytes 557088 | tf_op jit(solution)/shard_map/all_to_all | solution.py:344
  142.8 1.2 merge_far.1
  (2 shorter events, 0.0 us)
Async XLA Ops:
  1.8 47.2 %all-to-all-start = ((bf16[8,16,2176]{2,1,0:T(8,128)(2,1)}), bf16[8,16,2176]{2,1,0:T(8,128)(2,1)S(1)}, u32[]{:S(2)}, u32[]{:S(2)}) async-start(bf16[8,16,2176]{2,1,0:T(8,128)(2,1)} %pack.1), calls=%async_computation | async-start | bytes 1114112 | tf_op jit(solution)/shard_map/all_to_all | solution.py:293
  50.1 21.6 %copy-start = (bf16[32,64,256]{2,1,0:T(8,128)(2,1)S(1)}, bf16[32,64,256]{2,1,0:T(8,128)(2,1)}, u32[]{:S(2)}) copy-start(bf16[32,64,256]{2,1,0:T(8,128)(2,1)} %keys_ref.1) | copy-start | bytes 3145732
  50.1 21.6 %copy-start.1 = (bf16[32,64,256]{2,1,0:T(8,128)(2,1)S(1)}, bf16[32,64,256]{2,1,0:T(8,128)(2,1)}, u32[]{:S(2)}) copy-start(bf16[32,64,256]{2,1,0:T(8,128)(2,1)} %values_ref.1) | copy-start | bytes 3145732
  105.9 37.0 %all-to-all-start.3 = ((bf16[8,16,2176]{2,1,0:T(8,128)(2,1)}), bf16[8,16,2176]{2,1,0:T(8,128)(2,1)S(1)}, u32[]{:S(2)}, u32[]{:S(2)}) async-start(bf16[8,16,2176]{2,1,0:T(8,128)(2,1)} %bitcast.10), calls=%async_computation.3 | async-start | bytes 1114112 | tf_op jit(solution)/shard_map/all_to_all | solution.py:344

commit v4 on v3

--- a/solution.py
+++ b/solution.py
@@ -11,7 +11,7 @@
 FAR = 8
 PLANE = 8
 SLOT = 2
-BLOCK = 16
+BLOCK = 32
 DEAD = -1e30
 EXTRA = 128
 F32 = jnp.float32
@@ -132,37 +132,39 @@
     copy.wait()
     block = BLOCK
     blocks = cells // block
+    tile = 16
     token = iota((heads, hop_tok), 1)
     lane = iota((heads, cells), 1)
     zero = jnp.zeros((group, HEAD), F32)
-    nothing = jnp.zeros((heads, hop_tok), BF16)
 
     def pages(ref, cell):
-        return jnp.concatenate(
-            [ref[told_smem[which, cell + n]] for n in (0, 1) for which in (0, 1)], axis=0
-        )
+        return jnp.concatenate([ref[told_smem[which, cell]] for which in (0, 1)], axis=0)
 
     def scores(i):
         start = pl.multiple_of(i * block, block)
-        for head in range(heads):
-            query_ref[head * block : (head + 1) * block, :] = rows_ref[
-                pl.ds(start, block), head * HEAD : (head + 1) * HEAD
-            ].astype(F32)
-        for pair in range(0, block, 2):
-            spread = []
-            for cell in (pair, pair + 1):
-                query = query_ref[pl.ds(cell, heads, stride=block), :]
-                spread.append(jnp.concatenate([query[:group], zero], axis=1))
-                spread.append(jnp.concatenate([zero, query[group:]], axis=1))
-            both = lax.dot_general(
-                jnp.concatenate(spread, axis=0).astype(BF16),
-                pages(keys_ref, start + pair),
+        for sub in range(0, block, tile):
+            for head in range(heads):
+                to = sub * heads + head * tile
+                query_ref[to : to + tile, :] = rows_ref[
+                    pl.ds(start + sub, tile), head * HEAD : (head + 1) * HEAD
+                ].astype(F32)
+        for cell in range(block):
+            at = cell // tile * tile * heads + cell % tile
+            query = query_ref[pl.ds(at, heads, stride=tile), :]
+            spread = jnp.concatenate(
+                [
+                    jnp.concatenate([query[:group], zero], axis=1),
+                    jnp.concatenate([zero, query[group:]], axis=1),
+                ],
+                axis=0,
+            )
+            at = pl.multiple_of((start + cell) * heads, heads)
+            score_ref[pl.ds(at, heads), :] = lax.dot_general(
+                spread.astype(BF16),
+                pages(keys_ref, start + cell),
                 (((1,), (1,)), ((), ())),
                 preferred_element_type=F32,
             )
-            at = pl.multiple_of((start + pair) * heads, 2 * heads)
-            score_ref[pl.ds(at, heads), :] = both[:heads, :hop_tok]
-            score_ref[pl.ds(at + heads, heads), :] = both[heads:, hop_tok:]
 
     def softmax(i, carries):
         start = pl.multiple_of(i * block, block)
@@ -180,33 +182,36 @@
 
     def mix(i):
         start = pl.multiple_of(i * block, block)
-        for pair in range(0, block, 2):
-            at = pl.multiple_of((start + pair) * heads, 2 * heads)
-            one = jnp.concatenate([prob_ref[pl.ds(at, heads), :], nothing], axis=1)
-            two = jnp.concatenate([nothing, prob_ref[pl.ds(at + heads, heads), :]], axis=1)
-            both = jnp.dot(
-                jnp.concatenate([one, two], axis=0),
-                pages(values_ref, start + pair),
+        for cell in range(block):
+            at = pl.multiple_of((start + cell) * heads, heads)
+            mixed = jnp.dot(
+                prob_ref[pl.ds(at, heads), :],
+                pages(values_ref, start + cell),
                 preferred_element_type=F32,
             )
-            inverse = inverse_ref[pl.ds(at, 2 * heads), :]
-            for n in (0, 1):
-                low, mid, high = n * heads, n * heads + group, (n + 1) * heads
-                to = pair * heads
-                mixed_ref[to + low : to + mid, :] = both[low:mid, :HEAD] * inverse[low:mid]
-                mixed_ref[to + mid : to + high, :] = both[mid:high, HEAD:] * inverse[mid:high]
-        for head in range(heads):
-            out_ref[pl.ds(start, block), head * HEAD : (head + 1) * HEAD] = mixed_ref[
-                pl.ds(head, block, stride=heads), :
-            ].astype(BF16)
+            inverse = inverse_ref[pl.ds(at, heads), :]
+            to = cell * heads
+            mixed_ref[to : to + group, :] = mixed[:group, :HEAD] * inverse[:group]
+            mixed_ref[to + group : to + heads, :] = mixed[group:, HEAD:] * inverse[group:]
+        for sub in range(0, block, tile):
+            for head in range(heads):
+                out_ref[pl.ds(start + sub, tile), head * HEAD : (head + 1) * HEAD] = mixed_ref[
+                    pl.ds(sub * heads + head, tile, stride=heads), :
+                ].astype(BF16)
 
     def step(i, carries):
-        mix(jnp.maximum(i - 2, 0))
-        carries = softmax(jnp.clip(i - 1, 0, blocks - 1), carries)
-        scores(jnp.minimum(i, blocks - 1))
+        mix(i - 2)
+        carries = softmax(i - 1, carries)
+        scores(i)
         return carries
 
-    carries = lax.fori_loop(0, blocks + 2, step, jnp.zeros((heads, cells), F32))
+    scores(0)
+    carries = softmax(0, jnp.zeros((heads, cells), F32))
+    scores(1)
+    carries = lax.fori_loop(2, blocks, step, carries)
+    mix(blocks - 2)
+    carries = softmax(blocks - 1, carries)
+    mix(blocks - 1)
     told = jnp.concatenate(
         [*pieces(carries), jnp.zeros((EXTRA - 3 * heads, cells), F32)], axis=0
     )
@@ -226,25 +231,28 @@
     carries = (info[:heads] + info[heads : 2 * heads] + info[2 * heads : 3 * heads])[:, :cells]
     lane = iota((count, EXTRA), 1)
     told = jnp.zeros((count, EXTRA), F32)
+    some = jnp.max(sel_ref[...], axis=1, keepdims=True) > 0.0
     for head in range(heads):
         carry = jnp.broadcast_to(carries[head : head + 1], (count, cells))
-        high = jnp.max(jnp.where(chosen, carry, DEAD), axis=1, keepdims=True)
-        share = jnp.where(chosen, jnp.exp(jnp.minimum(carry - high, 0.0)), 0.0)
+        carry = jnp.where(chosen, carry, DEAD)
+        high = jnp.max(carry, axis=1, keepdims=True)
+        share = jnp.exp(carry - high)
         total = jnp.sum(share, axis=1, keepdims=True)
-        some = total > 0.0
-        share = share / jnp.where(some, total, 1.0)
+        share = share * (1.0 / total)
         major = share.astype(BF16)
-        minor = (share - major.astype(F32)).astype(BF16)
-        both = jnp.dot(
-            jnp.concatenate([major, minor], axis=0),
-            rows_ref[:, head * HEAD : (head + 1) * HEAD],
-            preferred_element_type=F32,
-        )
-        out_ref[:, head * HEAD : (head + 1) * HEAD] = (both[:count] + both[count:]).astype(BF16)
-        if not last:
-            carry = jnp.where(some, high + jnp.log(jnp.where(some, total, 1.0)), DEAD)
+        values = rows_ref[:, head * HEAD : (head + 1) * HEAD]
+        if last:
+            minor = (share - major.astype(F32)).astype(BF16)
+            both = jnp.dot(
+                jnp.concatenate([major, minor], axis=0), values, preferred_element_type=F32
+            )
+            merged = both[:count] + both[count:]
+        else:
+            merged = jnp.dot(major, values, preferred_element_type=F32)
+            carry = jnp.where(some, high + jnp.log(total), DEAD)
             for n, part in enumerate(pieces(carry)):
                 told = jnp.where(lane == n * heads + head, part, told)
+        out_ref[:, head * HEAD : (head + 1) * HEAD] = merged.astype(BF16)
     if not last:
         out_ref[:, width:] = told.astype(BF16)
 

time: 144 us -> 141 us (0.979)
  Pallas kernels: 18.5 us -> 14.7 us
    pallas_call x1, Pallas kernels: 11.7 us -> 8.45 us  [per_device(): pl.pallas_call(attend_kernel, out_shape=jax.ShapeDtypeStruct((cells, full...]
where the time goes in v4:
time: 141 us; the launch traced here: 140 us
  waiting for transfers between devices  65.3 us (46%)
  blocking collectives  41.3 us (29%)
  starting transfers between devices  18.9 us (13%)
  Pallas kernels  14.7 us (10%)
    all_to_all x1, waiting for transfers between devices, per_device(): lax.all_to_all(partial.reshape(far, req_dev, full), 'page', split_axis=0,...  32.7 us
    all_to_all x1, waiting for transfers between devices, per_device(): lax.all_to_all(rows, 'page', split_axis=0, concat_axis=0, axis_index_grou...  32.5 us
    all_to_all x1, blocking collectives, per_device(): lax.all_to_all(cell_rows.reshape(near, far * SLOT, full), 'page', split_a...  21.5 us
    all_to_all x1, blocking collectives, per_device(): lax.all_to_all(partial.reshape(near, far * SLOT, full), 'page', split_axi...  19.8 us
    all_to_all x1, starting transfers between devices, per_device(): lax.all_to_all(rows, 'page', split_axis=0, concat_axis=0, axis_index_grou...  14.7 us
    pallas_call x1, Pallas kernels, per_device(): pl.pallas_call(attend_kernel, out_shape=jax.ShapeDtypeStruct((cells, full...  8.45 us
    all_to_all x1, starting transfers between devices, per_device(): lax.all_to_all(partial.reshape(far, req_dev, full), 'page', split_axis=0,...  4.23 us
  transfers between devices with their start and end apart: 2, of which 2 were waited for; matrix products, arithmetic and copies ran while one was open for 0% of the time, Pallas kernels for 0%

profile of v4, /device:TPU:24, one launch (start us, length us, event | category | flops | bytes accessed | tf_op | source)
XLA Modules:
  0.0 140.3 jit_solution(892321522292905270)
XLA Ops:
  0.0 1.8 %pack.1 = bf16[8,16,2176]{2,1,0:T(8,128)(2,1)} custom-call(bf16[16,2048]{1,0:T(8,128)(2,1)} %queries_in.1, s32[8,16]{1,0:T(8,128)} %bitcast.20, s32[16,16]{1,0:T(8,128)} %bitcast.19, s32[1,16]{1,0:T(1,128)} %bitcast.21), custom_call_target="tpu_custom_call" | custom-call | tf_op jit(solution)/shard_map/pack/pallas_call | solution.py:280
  1.8 14.7 %all-to-all-start = ((bf16[8,16,2176]{2,1,0:T(8,128)(2,1)}), bf16[8,16,2176]{2,1,0:T(8,128)(2,1)S(1)}, u32[]{:S(2)}, u32[]{:S(2)}) async-start(bf16[8,16,2176]{2,1,0:T(8,128)(2,1)} %pack.1), calls=%async_computation | async-start | bytes 1114112 | tf_op jit(solution)/shard_map/all_to_all | solution.py:301
  16.4 32.5 %all-to-all-done = bf16[8,16,2176]{2,1,0:T(8,128)(2,1)S(1)} async-done(((bf16[8,16,2176]{2,1,0:T(8,128)(2,1)}), bf16[8,16,2176]{2,1,0:T(8,128)(2,1)S(1)}, u32[]{:S(2)}, u32[]{:S(2)}) %all-to-all-start) | async-done | bytes 557088 | tf_op jit(solution)/shard_map/all_to_all | solution.py:301
  49.0 1.1 select.7
  50.1 0.0 copy-start
  50.1 0.0 copy-start.1
  50.1 21.5 %all_to_all.20 = bf16[16,16,2176]{2,1,0:T(8,128)(2,1)S(1)} all-to-all(bf16[16,16,2176]{2,1,0:T(8,128)(2,1)S(1)} %bitcast.18), channel_id=1, replica_groups={{0,4,8,12,16,20,24,28,32,36,40,44,48,52,56,60},{64,68,72,76,80,84,88,92..., dimensions={0} | all-to-all | bytes 2228224 | tf_op jit(solution)/shard_map/all_to_all | solution.py:317
  71.6 0.0 copy-done
  71.6 0.0 copy-done.1
  71.6 8.5 %attend.1 = bf16[256,2176]{1,0:T(8,128)(2,1)S(1)} custom-call(bf16[256,2176]{1,0:T(8,128)(2,1)S(1)} %bitcast.14, bf16[32,64,256]{2,1,0:T(8,128)(2,1)S(1)} %copy-done, bf16[32,64,256]{2,1,0:T(8,128)(2,1)S(1)} %copy-done.1), custom_call_target="tpu_custom_call" | custom-call | tf_op jit(solution)/shard_map/attend/pallas_call | solution.py:321
  80.1 19.8 %all_to_all.21 = bf16[16,16,2176]{2,1,0:T(8,128)(2,1)S(1)} all-to-all(bf16[16,16,2176]{2,1,0:T(8,128)(2,1)S(1)} %bitcast.15), channel_id=1, replica_groups={{0,4,8,12,16,20,24,28,32,36,40,44,48,52,56,60},{64,68,72,76,80,84,88,92..., dimensions={0} | all-to-all | bytes 2228224 | tf_op jit(solution)/shard_map/all_to_all | solution.py:339
  99.9 2.2 %merge_near.1 = bf16[128,2176]{1,0:T(8,128)(2,1)} custom-call(bf16[256,2176]{1,0:T(8,128)(2,1)S(1)} %bitcast.13, f32[128,256]{1,0:T(8,128)S(1)} %get-tuple-element.8.sel_ref), custom_call_target="tpu_custom_call" | custom-call | tf_op jit(solution)/shard_map/merge_near/pallas_call | solution.py:344
  102.1 4.2 %all-to-all-start.3 = ((bf16[8,16,2176]{2,1,0:T(8,128)(2,1)}), bf16[8,16,2176]{2,1,0:T(8,128)(2,1)S(1)}, u32[]{:S(2)}, u32[]{:S(2)}) async-start(bf16[8,16,2176]{2,1,0:T(8,128)(2,1)} %bitcast.10), calls=%async_computation.3 | async-start | bytes 1114112 | tf_op jit(solution)/shard_map/all_to_all | solution.py:352
  106.3 32.7 %all-to-all-done.3 = bf16[8,16,2176]{2,1,0:T(8,128)(2,1)S(1)} async-done(((bf16[8,16,2176]{2,1,0:T(8,128)(2,1)}), bf16[8,16,2176]{2,1,0:T(8,128)(2,1)S(1)}, u32[]{:S(2)}, u32[]{:S(2)}) %all-to-all-start.3) | async-done | bytes 557088 | tf_op jit(solution)/shard_map/all_to_all | solution.py:352
  139.1 1.2 merge_far.1
  (2 shorter events, 0.0 us)
Async XLA Ops:
  1.8 47.2 %all-to-all-start = ((bf16[8,16,2176]{2,1,0:T(8,128)(2,1)}), bf16[8,16,2176]{2,1,0:T(8,128)(2,1)S(1)}, u32[]{:S(2)}, u32[]{:S(2)}) async-start(bf16[8,16,2176]{2,1,0:T(8,128)(2,1)} %pack.1), calls=%async_computation | async-start | bytes 1114112 | tf_op jit(solution)/shard_map/all_to_all | solution.py:301
  50.1 21.6 %copy-start = (bf16[32,64,256]{2,1,0:T(8,128)(2,1)S(1)}, bf16[32,64,256]{2,1,0:T(8,128)(2,1)}, u32[]{:S(2)}) copy-start(bf16[32,64,256]{2,1,0:T(8,128)(2,1)} %keys_ref.1) | copy-start | bytes 3145732
  50.1 21.6 %copy-start.1 = (bf16[32,64,256]{2,1,0:T(8,128)(2,1)S(1)}, bf16[32,64,256]{2,1,0:T(8,128)(2,1)}, u32[]{:S(2)}) copy-start(bf16[32,64,256]{2,1,0:T(8,128)(2,1)} %values_ref.1) | copy-start | bytes 3145732
  102.1 37.0 %all-to-all-start.3 = ((bf16[8,16,2176]{2,1,0:T(8,128)(2,1)}), bf16[8,16,2176]{2,1,0:T(8,128)(2,1)S(1)}, u32[]{:S(2)}, u32[]{:S(2)}) async-start(bf16[8,16,2176]{2,1,0:T(8,128)(2,1)} %bitcast.10), calls=%async_computation.3 | async-start | bytes 1114112 | tf_op jit(solution)/shard_map/all_to_all | solution.py:352

commit v5 on v4

v5 whole, which is shorter than its diff:
```python
import functools

import jax
import jax.numpy as jnp
from jax import lax
from jax.experimental import pallas as pl
from jax.experimental.pallas import tpu as pltpu
from jax.sharding import PartitionSpec as P

HEAD = 128
LANES = 128
FAR = 8
PLANE = 8
SLOT = 2
TILE = 16
EXTRA = 8
BLOCK = 32
DEAD = -1e30
F32 = jnp.float32
BF16 = jnp.bfloat16


def iota(shape, dim):
    return lax.broadcasted_iota(jnp.int32, shape, dim)


def pieces(x):
    high = x.astype(BF16).astype(F32)
    mid = (x - high).astype(BF16).astype(F32)
    low = (x - high - mid).astype(BF16).astype(F32)
    return high, mid, low


def arrange(parts):
    lane = iota((EXTRA, LANES), 1) // TILE
    out = jnp.zeros((EXTRA, LANES), F32)
    for n, (x, group) in enumerate(parts):
        shift = (n - group) * TILE % LANES
        out = jnp.where(lane == n, pltpu.roll(x, shift, 1) if shift else x, out)
    return out


def extra_of(ref, n):
    return ref[n, ref.shape[1] - EXTRA :, :].astype(F32)


def put_extra(ref, n, x):
    ref[n, ref.shape[1] - EXTRA :, :] = x.astype(BF16)


def put_carries(ref, columns):
    wide = LANES // TILE
    for n in range(ref.shape[0]):
        at = n // wide * LANES
        put_extra(
            ref,
            n,
            arrange(
                [
                    (columns[v : v + EXTRA, at : at + LANES], n % wide)
                    for v in range(0, columns.shape[0], EXTRA)
                ]
            ),
        )


def get_carries(ref, heads):
    wide = LANES // TILE
    sums = []
    for n in range(ref.shape[0]):
        x = extra_of(ref, n)
        sums.append(
            x + pltpu.roll(x, LANES - heads // EXTRA * TILE, 1)
            + pltpu.roll(x, LANES - 2 * (heads // EXTRA) * TILE, 1)
        )
    return jnp.concatenate(
        [
            jnp.concatenate(
                [
                    arrange([(x, group) for x in sums[at : at + wide]])
                    for at in range(0, len(sums), wide)
                ],
                axis=1,
            )
            for group in range(heads // EXTRA)
        ],
        axis=0,
    )


def pack_kernel(
    hop_tok, queries_in, routes_in, tables_in, lengths_in, out_ref,
    queries_ref, routes_ref, tables_ref, lengths_ref, sems,
):
    far = out_ref.shape[0]
    hops, req_dev = routes_ref.shape
    copies = [
        pltpu.make_async_copy(a, b, sems.at[n])
        for n, (a, b) in enumerate(
            [
                (queries_in, queries_ref),
                (routes_in, routes_ref),
                (tables_in, tables_ref),
                (lengths_in, lengths_ref),
            ]
        )
    ]
    for copy in copies:
        copy.start()
    for copy in copies:
        copy.wait()
    live = jnp.clip(lengths_ref[...] - iota((hops, req_dev), 0) * hop_tok, 0, hop_tok)
    kinds = [
        routes_ref[...],
        live,
        tables_ref[pl.ds(0, hops, stride=2), :],
        tables_ref[pl.ds(1, hops, stride=2), :],
    ]
    blank = jnp.zeros((hops, LANES - req_dev), F32)
    told = arrange([(jnp.concatenate([x.astype(F32), blank], axis=1), 0) for x in kinds])
    for n in range(far):
        for head in range(queries_ref.shape[1] // HEAD):
            out_ref[n, head * TILE : (head + 1) * TILE, :] = queries_ref[
                :, head * HEAD : (head + 1) * HEAD
            ]
        put_extra(out_ref, n, told)


def select_kernel(base_ref, rows_ref, out_ref, sel_ref):
    far, near = rows_ref.shape[0], out_ref.shape[0]
    heads = (rows_ref.shape[1] - EXTRA) // TILE
    count, cells = far * TILE, near * TILE
    hops = EXTRA
    told = [extra_of(rows_ref, n) for n in range(far)]
    routes, live, first, second = [arrange([(x, kind) for x in told]) for kind in range(4)]
    coded = first + 32.0 * second + 1024.0 * live
    info = jnp.concatenate([routes, coded, jnp.zeros((LANES - 2 * hops, LANES), F32)], axis=0).T
    lane = iota((count, cells), 1)
    row = iota((count, cells), 0)
    dest = (lane // TILE + base_ref[0]).astype(F32)
    own = (lane // SLOT) % far == row // TILE
    named = jnp.zeros((count, cells), F32)
    code = jnp.zeros((count, cells), F32)
    for hop in range(hops):
        hit = (info[:, hop : hop + 1] == dest) & own
        named = jnp.where(hit, 1.0, named)
        code = jnp.where(hit, info[:, hops + hop : hops + hop + 1], code)
    a = iota((count, count), 0)
    b = iota((count, count), 1)
    before = jnp.where((a // TILE == b // TILE) & (b < a), 1.0, 0.0).astype(BF16)
    rank = jnp.dot(before, named.astype(BF16), preferred_element_type=F32)
    sel = jnp.where(rank == (lane % SLOT).astype(F32), named, 0.0)
    sel_ref[...] = sel
    code = jnp.sum(sel * code, axis=0, keepdims=True)
    live = jnp.floor(code * (1.0 / 1024.0))
    code = code - 1024.0 * live
    second = jnp.floor(code * (1.0 / 32.0))
    first = code - 32.0 * second
    told = jnp.concatenate([first, second, live, jnp.zeros((EXTRA - 3, cells), F32)], axis=0)
    wide = LANES // TILE
    for n in range(near):
        at = n // wide * LANES
        put_extra(out_ref, n, arrange([(told[:, at : at + LANES], n % wide)]))
    place = sel.T.astype(BF16)
    for head in range(0, heads, 2):
        at = head * TILE
        both = jnp.concatenate(
            [
                rows_ref[:, at : at + TILE, :].reshape(count, HEAD),
                rows_ref[:, at + TILE : at + 2 * TILE, :].reshape(count, HEAD),
            ],
            axis=1,
        )
        both = jnp.dot(place, both, preferred_element_type=F32).astype(BF16)
        out_ref[:, at : at + TILE, :] = both[:, :HEAD].reshape(near, TILE, HEAD)
        out_ref[:, at + TILE : at + 2 * TILE, :] = both[:, HEAD:].reshape(near, TILE, HEAD)


def attend_kernel(
    rows_ref,
    keys_ref,
    values_ref,
    out_ref,
    told_ref,
    told_smem,
    query_ref,
    score_ref,
    prob_ref,
    inverse_ref,
    mixed_ref,
    sem,
):
    near = rows_ref.shape[0]
    heads = (rows_ref.shape[1] - EXTRA) // TILE
    cells = near * TILE
    group = heads // 2
    hop_tok = 2 * keys_ref.shape[1]
    scale = HEAD ** -0.5
    wide = LANES // TILE
    for at in range(0, near, wide):
        told_ref[:, at * TILE : at * TILE + LANES] = arrange(
            [(extra_of(rows_ref, at + n), 0) for n in range(wide)]
        ).astype(jnp.int32)
    copy = pltpu.make_async_copy(told_ref, told_smem, sem)
    copy.start()
    copy.wait()
    block = BLOCK
    blocks = cells // block
    token = iota((heads, hop_tok), 1)
    lane = iota((heads, cells), 1)
    zero = jnp.zeros((group, HEAD), F32)

    def pages(ref, cell):
        return jnp.concatenate([ref[told_smem[which, cell]] for which in (0, 1)], axis=0)

    def scores(i):
        start = pl.multiple_of(i * block, block)
        for sub in range(0, block, TILE):
            query_ref[sub * heads : (sub + TILE) * heads, :] = rows_ref[
                i * (block // TILE) + sub // TILE, : heads * TILE, :
            ].astype(F32)
        for cell in range(block):
            at = cell // TILE * TILE * heads + cell % TILE
            query = query_ref[pl.ds(at, heads, stride=TILE), :]
            spread = jnp.concatenate(
                [
                    jnp.concatenate([query[:group], zero], axis=1),
                    jnp.concatenate([zero, query[group:]], axis=1),
                ],
                axis=0,
            )
            at = pl.multiple_of((start + cell) * heads, heads)
            score_ref[pl.ds(at, heads), :] = lax.dot_general(
                spread.astype(BF16),
                pages(keys_ref, start + cell),
                (((1,), (1,)), ((), ())),
                preferred_element_type=F32,
            )

    def softmax(i, carries):
        start = pl.multiple_of(i * block, block)
        for cell in range(block):
            at = pl.multiple_of((start + cell) * heads, heads)
            own = score_ref[pl.ds(at, heads), :] * scale
            own = jnp.where(token < told_smem[2, start + cell], own, DEAD)
            top = jnp.max(own, axis=1, keepdims=True)
            probs = jnp.exp(own - top)
            total = jnp.sum(probs, axis=1, keepdims=True)
            carries = jnp.where(lane == start + cell, top + jnp.log(total), carries)
            prob_ref[pl.ds(at, heads), :] = probs.astype(BF16)
            inverse_ref[pl.ds(at, heads), :] = jnp.broadcast_to(1.0 / total, (heads, HEAD))
        return carries

    def mix(i):
        start = pl.multiple_of(i * block, block)
        for cell in range(block):
            at = pl.multiple_of((start + cell) * heads, heads)
            mixed = jnp.dot(
                prob_ref[pl.ds(at, heads), :],
                pages(values_ref, start + cell),
                preferred_element_type=F32,
            )
            inverse = inverse_ref[pl.ds(at, heads), :]
            to = cell * heads
            mixed_ref[to : to + group, :] = mixed[:group, :HEAD] * inverse[:group]
            mixed_ref[to + group : to + heads, :] = mixed[group:, HEAD:] * inverse[group:]
        for sub in range(0, block, TILE):
            for head in range(heads):
                out_ref[
                    i * (block // TILE) + sub // TILE, head * TILE : (head + 1) * TILE, :
                ] = mixed_ref[pl.ds(sub * heads + head, TILE, stride=heads), :].astype(BF16)

    def step(i, carries):
        mix(i - 2)
        carries = softmax(i - 1, carries)
        scores(i)
        return carries

    scores(0)
    carries = softmax(0, jnp.zeros((heads, cells), F32))
    scores(1)
    carries = lax.fori_loop(2, blocks, step, carries)
    mix(blocks - 2)
    carries = softmax(blocks - 1, carries)
    mix(blocks - 1)
    put_carries(out_ref, jnp.concatenate(pieces(carries), axis=0))


def merge_kernel(last, rows_ref, sel_ref, out_ref):
    heads = (rows_ref.shape[1] - EXTRA) // TILE
    cells = rows_ref.shape[0] * TILE
    count = sel_ref.shape[0]
    chosen = sel_ref[...] > 0.0
    carries = get_carries(rows_ref, heads)
    lane = iota((count, LANES), 1)
    told = jnp.zeros((count, LANES), F32)
    some = jnp.max(sel_ref[...], axis=1, keepdims=True) > 0.0
    for head in range(heads):
        carry = jnp.broadcast_to(carries[head : head + 1], (count, cells))
        carry = jnp.where(chosen, carry, DEAD)
        high = jnp.max(carry, axis=1, keepdims=True)
        share = jnp.exp(carry - high)
        total = jnp.sum(share, axis=1, keepdims=True)
        share = share * (1.0 / total)
        major = share.astype(BF16)
        values = rows_ref[:, head * TILE : (head + 1) * TILE, :].reshape(cells, HEAD)
        if last:
            minor = (share - major.astype(F32)).astype(BF16)
            both = jnp.dot(
                jnp.concatenate([major, minor], axis=0), values, preferred_element_type=F32
            )
            merged = both[:count] + both[count:]
            out_ref[:, head * HEAD : (head + 1) * HEAD] = merged.astype(BF16)
        else:
            merged = jnp.dot(major, values, preferred_element_type=F32)
            out_ref[:, head * TILE : (head + 1) * TILE, :] = merged.astype(BF16).reshape(
                count // TILE, TILE, HEAD
            )
            carry = jnp.where(some, high + jnp.log(total), DEAD)
            for n, part in enumerate(pieces(carry)):
                told = jnp.where(lane == n * heads + head, part, told)
    if not last:
        put_carries(out_ref, told.T[: 3 * heads])


def far_sets(far, near):
    turn = [[m ^ PLANE if n >= far // 2 else m for m in range(near)] for n in range(far)]
    return [[n * near + turn[n][m] for n in range(far)] for m in range(near)]


def per_device(queries, cache_keys, cache_values, routes, page_table, lengths):
    pages = lax.axis_size("page")
    far, near = FAR, pages // FAR
    near_groups = [[n * near + m for m in range(near)] for n in range(far)]
    far_groups = far_sets(far, near)
    req_dev, hops = routes.shape
    width = queries.shape[1]
    heads = width // HEAD
    hop_tok = page_table.shape[2] * cache_keys.shape[1]
    cells = near * far * SLOT
    count = far * req_dev
    tall = heads * TILE + EXTRA
    vmem = pl.BlockSpec(memory_space=pltpu.VMEM)
    params = pltpu.CompilerParams(vmem_limit_bytes=48 * 1024 * 1024)

    def exchange(x, groups):
        return lax.all_to_all(
            x, "page", split_axis=0, concat_axis=0, axis_index_groups=groups, tiled=True
        )

    rows = pl.pallas_call(
        functools.partial(pack_kernel, hop_tok),
        out_shape=jax.ShapeDtypeStruct((far, tall, HEAD), BF16),
        in_specs=[pl.BlockSpec(memory_space=pl.ANY)] * 4,
        out_specs=vmem,
        scratch_shapes=[
            pltpu.VMEM((req_dev, width), BF16),
            pltpu.VMEM((hops, req_dev), jnp.int32),
            pltpu.VMEM((hops * page_table.shape[2], req_dev), jnp.int32),
            pltpu.VMEM((1, req_dev), jnp.int32),
            pltpu.SemaphoreType.DMA((4,)),
        ],
        compiler_params=pltpu.CompilerParams(vmem_limit_bytes=60 * 1024 * 1024),
        name="pack",
    )(
        queries,
        routes.T,
        page_table.transpose(1, 2, 0).reshape(-1, req_dev),
        lengths.reshape(1, req_dev),
    )
    rows = exchange(rows, far_groups)
    base = (lax.axis_index("page") // near * near).astype(jnp.int32).reshape(1)
    cell_rows, sel = pl.pallas_call(
        select_kernel,
        out_shape=(
            jax.ShapeDtypeStruct((near, tall, HEAD), BF16),
            jax.ShapeDtypeStruct((count, cells), F32),
        ),
        in_specs=[pl.BlockSpec(memory_space=pltpu.SMEM), vmem],
        out_specs=(vmem, vmem),
        compiler_params=params,
        name="select",
    )(base, rows)
    cell_rows = exchange(cell_rows, near_groups)
    partial = pl.pallas_call(
        attend_kernel,
        out_shape=jax.ShapeDtypeStruct((near, tall, HEAD), BF16),
        in_specs=[vmem] * 3,
        out_specs=vmem,
        scratch_shapes=[
            pltpu.VMEM((8, cells), jnp.int32),
            pltpu.SMEM((8, cells), jnp.int32),
            pltpu.VMEM((BLOCK * heads, HEAD), F32),
            pltpu.VMEM((cells * heads, HEAD), F32),
            pltpu.VMEM((cells * heads, HEAD), BF16),
            pltpu.VMEM((cells * heads, HEAD), F32),
            pltpu.VMEM((BLOCK * heads, HEAD), F32),
            pltpu.SemaphoreType.DMA,
        ],
        compiler_params=params,
        name="attend",
    )(cell_rows, cache_keys, cache_values)
    partial = exchange(partial, near_groups)
    partial = pl.pallas_call(
        functools.partial(merge_kernel, False),
        out_shape=jax.ShapeDtypeStruct((far, tall, HEAD), BF16),
        in_specs=[vmem] * 2,
        out_specs=vmem,
        compiler_params=params,
        name="merge_near",
    )(partial, sel)
    partial = exchange(partial, far_groups)
    mine = (
        jnp.arange(count, dtype=jnp.int32)[None, :] % req_dev
        == jnp.arange(req_dev, dtype=jnp.int32)[:, None]
    ).astype(F32)
    return pl.pallas_call(
        functools.partial(merge_kernel, True),
        out_shape=jax.ShapeDtypeStruct((req_dev, width), BF16),
        in_specs=[vmem] * 2,
        out_specs=vmem,
        compiler_params=params,
        name="merge_far",
    )(partial, mine)


def solution(mesh):
    placed = (
        P("page", "mp"),
        P("page", None, "mp"),
        P("page", None, "mp"),
        P("page", None),
        P("page", None, None),
        P("page"),
    )
    return jax.shard_map(
        per_device, mesh=mesh, in_specs=placed, out_specs=P("page", "mp"), check_vma=False
    )
```

time: 141 us -> 139 us (0.986)
  waiting for transfers between devices: 65.3 us -> 63.8 us
    all_to_all x2, waiting for transfers between devices: 65.3 us -> 63.8 us  [exchange(): lax.all_to_all(x, 'page', split_axis=0, concat_axis=0, axis_index_groups=...]
where the time goes in v5:
time: 139 us
  waiting for transfers between devices  63.8 us (46%)
  blocking collectives  40.9 us (29%)
  starting transfers between devices  19 us (14%)
  Pallas kernels  15.1 us (11%)
    all_to_all x2, waiting for transfers between devices, exchange(): lax.all_to_all(x, 'page', split_axis=0, concat_axis=0, axis_index_groups=...  63.8 us
    all_to_all x2, blocking collectives, exchange(): lax.all_to_all(x, 'page', split_axis=0, concat_axis=0, axis_index_groups=...  40.9 us
    all_to_all x2, starting transfers between devices, exchange(): lax.all_to_all(x, 'page', split_axis=0, concat_axis=0, axis_index_groups=...  19 us
    pallas_call x1, Pallas kernels, per_device(): pl.pallas_call(attend_kernel, out_shape=jax.ShapeDtypeStruct((near, tall,...  8.55 us
  transfers between devices with their start and end apart: 2, of which 2 were waited for; matrix products, arithmetic and copies ran while one was open for 0% of the time, Pallas kernels for 0%

profile of v5, /device:TPU:24, one launch (start us, length us, event | category | flops | bytes accessed | tf_op | source)
XLA Modules:
  0.0 138.9 jit_solution(16401271240061445188)
XLA Ops:
  0.0 1.8 %pack.1 = bf16[8,264,128]{2,1,0:T(8,128)(2,1)} custom-call(bf16[16,2048]{1,0:T(8,128)(2,1)} %queries_in.1, s32[8,16]{1,0:T(8,128)} %bitcast.7, s32[16,16]{1,0:T(8,128)} %bitcast.6, s32[1,16]{1,0:T(1,128)} %bitcast.8), custom_call_target="tpu_custom_call" | custom-call | tf_op jit(solution)/shard_map/pack/pallas_call | solution.py:351
  1.8 14.7 %all-to-all-start = ((bf16[8,264,128]{2,1,0:T(8,128)(2,1)}), bf16[8,264,128]{2,1,0:T(8,128)(2,1)S(1)}, u32[]{:S(2)}, u32[]{:S(2)}) async-start(bf16[8,264,128]{2,1,0:T(8,128)(2,1)} %pack.1), calls=%async_computation | async-start | bytes 1081344 | tf_op jit(solution)/shard_map/all_to_all | solution.py:347
  16.4 31.7 %all-to-all-done.rows_ref = bf16[8,264,128]{2,1,0:T(8,128)(2,1)S(1)} async-done(((bf16[8,264,128]{2,1,0:T(8,128)(2,1)}), bf16[8,264,128]{2,1,0:T(8,128)(2,1)S(1)}, u32[]{:S(2)}, u32[]{:S(2)}) %all-to-all-start) | async-done | bytes 540704 | tf_op jit(solution)/shard_map/all_to_all | solution.py:347
  48.2 1.1 select.7
  49.3 0.0 copy-start
  49.3 0.0 copy-start.1
  49.3 21.3 %all_to_all.20.rows_ref = bf16[16,264,128]{2,1,0:T(8,128)(2,1)S(1)} all-to-all(bf16[16,264,128]{2,1,0:T(8,128)(2,1)S(1)} %get-tuple-element.7), channel_id=1, replica_groups={{0,4,8,12,16,20,24,28,32,36,40,44,48,52,56,60},{64,68,72,76,80,84,88,92..., dimensions={0} | all-to-all | bytes 2162688 | tf_op jit(solution)/shard_map/all_to_all | solution.py:347
  70.6 0.0 copy-done
  70.6 0.0 copy-done.1
  70.6 8.5 %attend.1 = bf16[16,264,128]{2,1,0:T(8,128)(2,1)S(1)} custom-call(bf16[16,264,128]{2,1,0:T(8,128)(2,1)S(1)} %all_to_all.20.rows_ref, bf16[32,64,256]{2,1,0:T(8,128)(2,1)S(1)} %copy-done, bf16[32,64,256]{2,1,0:T(8,128)(2,1)S(1)} %copy-done.1), custom_call_target="tpu_custom_call" | custom-call | tf_op jit(solution)/shard_map/attend/pallas_call | solution.py:385
  79.2 19.6 %all_to_all.21.rows_ref = bf16[16,264,128]{2,1,0:T(8,128)(2,1)S(1)} all-to-all(bf16[16,264,128]{2,1,0:T(8,128)(2,1)S(1)} %attend.1), channel_id=1, replica_groups={{0,4,8,12,16,20,24,28,32,36,40,44,48,52,56,60},{64,68,72,76,80,84,88,92..., dimensions={0} | all-to-all | bytes 2162688 | tf_op jit(solution)/shard_map/all_to_all | solution.py:347
  98.8 2.4 %merge_near.1 = bf16[8,264,128]{2,1,0:T(8,128)(2,1)} custom-call(bf16[16,264,128]{2,1,0:T(8,128)(2,1)S(1)} %all_to_all.21.rows_ref, f32[128,256]{1,0:T(8,128)S(1)} %get-tuple-element.8.sel_ref), custom_call_target="tpu_custom_call" | custom-call | tf_op jit(solution)/shard_map/merge_near/pallas_call | solution.py:404
  101.2 4.3 %all-to-all-start.3 = ((bf16[8,264,128]{2,1,0:T(8,128)(2,1)}), bf16[8,264,128]{2,1,0:T(8,128)(2,1)S(1)}, u32[]{:S(2)}, u32[]{:S(2)}) async-start(bf16[8,264,128]{2,1,0:T(8,128)(2,1)} %merge_near.1), calls=%async_computation.3 | async-start | bytes 1081344 | tf_op jit(solution)/shard_map/all_to_all | solution.py:347
  105.6 32.0 %all-to-all-done.3.rows_ref = bf16[8,264,128]{2,1,0:T(8,128)(2,1)S(1)} async-done(((bf16[8,264,128]{2,1,0:T(8,128)(2,1)}), bf16[8,264,128]{2,1,0:T(8,128)(2,1)S(1)}, u32[]{:S(2)}, u32[]{:S(2)}) %all-to-all-start.3) | async-done | bytes 540704 | tf_op jit(solution)/shard_map/all_to_all | solution.py:347
  137.6 1.3 merge_far.1
  (2 shorter events, 0.0 us)
Async XLA Ops:
  1.8 46.4 %all-to-all-start = ((bf16[8,264,128]{2,1,0:T(8,128)(2,1)}), bf16[8,264,128]{2,1,0:T(8,128)(2,1)S(1)}, u32[]{:S(2)}, u32[]{:S(2)}) async-start(bf16[8,264,128]{2,1,0:T(8,128)(2,1)} %pack.1), calls=%async_computation | async-start | bytes 1081344 | tf_op jit(solution)/shard_map/all_to_all | solution.py:347
  49.3 21.4 %copy-start = (bf16[32,64,256]{2,1,0:T(8,128)(2,1)S(1)}, bf16[32,64,256]{2,1,0:T(8,128)(2,1)}, u32[]{:S(2)}) copy-start(bf16[32,64,256]{2,1,0:T(8,128)(2,1)} %keys_ref.1) | copy-start | bytes 3145732
  49.3 21.3 %copy-start.1 = (bf16[32,64,256]{2,1,0:T(8,128)(2,1)S(1)}, bf16[32,64,256]{2,1,0:T(8,128)(2,1)}, u32[]{:S(2)}) copy-start(bf16[32,64,256]{2,1,0:T(8,128)(2,1)} %values_ref.1) | copy-start | bytes 3145732
  101.2 36.4 %all-to-all-start.3 = ((bf16[8,264,128]{2,1,0:T(8,128)(2,1)}), bf16[8,264,128]{2,1,0:T(8,128)(2,1)S(1)}, u32[]{:S(2)}, u32[]{:S(2)}) async-start(bf16[8,264,128]{2,1,0:T(8,128)(2,1)} %merge_near.1), calls=%async_computation.3 | async-start | bytes 1081344 | tf_op jit(solution)/shard_map/all_to_all | solution.py:347

commit v6 on v5

--- a/solution.py
+++ b/solution.py
@@ -10,7 +10,6 @@
 HEAD = 128
 LANES = 128
 FAR = 8
-PLANE = 8
 SLOT = 2
 TILE = 16
 EXTRA = 8
@@ -92,7 +91,6 @@
     hop_tok, queries_in, routes_in, tables_in, lengths_in, out_ref,
     queries_ref, routes_ref, tables_ref, lengths_ref, sems,
 ):
-    far = out_ref.shape[0]
     hops, req_dev = routes_ref.shape
     copies = [
         pltpu.make_async_copy(a, b, sems.at[n])
@@ -118,12 +116,11 @@
     ]
     blank = jnp.zeros((hops, LANES - req_dev), F32)
     told = arrange([(jnp.concatenate([x.astype(F32), blank], axis=1), 0) for x in kinds])
-    for n in range(far):
-        for head in range(queries_ref.shape[1] // HEAD):
-            out_ref[n, head * TILE : (head + 1) * TILE, :] = queries_ref[
-                :, head * HEAD : (head + 1) * HEAD
-            ]
-        put_extra(out_ref, n, told)
+    for head in range(queries_ref.shape[1] // HEAD):
+        out_ref[head * TILE : (head + 1) * TILE, :] = queries_ref[
+            :, head * HEAD : (head + 1) * HEAD
+        ]
+    out_ref[out_ref.shape[0] - EXTRA :, :] = told.astype(BF16)
 
 
 def select_kernel(base_ref, rows_ref, out_ref, sel_ref):
@@ -323,16 +320,11 @@
         put_carries(out_ref, told.T[: 3 * heads])
 
 
-def far_sets(far, near):
-    turn = [[m ^ PLANE if n >= far // 2 else m for m in range(near)] for n in range(far)]
-    return [[n * near + turn[n][m] for n in range(far)] for m in range(near)]
-
-
 def per_device(queries, cache_keys, cache_values, routes, page_table, lengths):
     pages = lax.axis_size("page")
     far, near = FAR, pages // FAR
     near_groups = [[n * near + m for m in range(near)] for n in range(far)]
-    far_groups = far_sets(far, near)
+    far_groups = [[n * near + m for n in range(far)] for m in range(near)]
     req_dev, hops = routes.shape
     width = queries.shape[1]
     heads = width // HEAD
@@ -350,7 +342,7 @@
 
     rows = pl.pallas_call(
         functools.partial(pack_kernel, hop_tok),
-        out_shape=jax.ShapeDtypeStruct((far, tall, HEAD), BF16),
+        out_shape=jax.ShapeDtypeStruct((tall, HEAD), BF16),
         in_specs=[pl.BlockSpec(memory_space=pl.ANY)] * 4,
         out_specs=vmem,
         scratch_shapes=[
@@ -368,7 +360,7 @@
         page_table.transpose(1, 2, 0).reshape(-1, req_dev),
         lengths.reshape(1, req_dev),
     )
-    rows = exchange(rows, far_groups)
+    rows = lax.all_gather(rows, "page", axis_index_groups=far_groups)
     base = (lax.axis_index("page") // near * near).astype(jnp.int32).reshape(1)
     cell_rows, sel = pl.pallas_call(
         select_kernel,

time: 139 us -> 135 us (0.971)
  blocking collectives: 40.9 us -> 79.2 us
  waiting for transfers between devices: 63.8 us -> 32 us
  starting transfers between devices: 19 us -> 7.51 us
    all_gather x0 -> x1, blocking collectives: none -> 37.3 us  [per_device(): rows = lax.all_gather(rows, 'page', axis_index_groups=far_groups)]
    all_to_all x2 -> x1, waiting for transfers between devices: 63.8 us -> 32 us  [exchange(): lax.all_to_all(x, 'page', split_axis=0, concat_axis=0, axis_index_groups=...]
    all_to_all x2 -> x1, starting transfers between devices: 19 us -> 7.51 us  [exchange(): lax.all_to_all(x, 'page', split_axis=0, concat_axis=0, axis_index_groups=...]
  transfers between devices with their start and end apart: 2 -> 1, of which waited for: 2 -> 1; matrix products, arithmetic and copies ran while one was open for 0% -> 0% of each run, Pallas kernels for 0% -> 0%
where the time goes in v6:
time: 135 us; the launch traced here: 134 us
  blocking collectives  79.2 us (59%)
  waiting for transfers between devices  32 us (24%)
  Pallas kernels  14.9 us (11%)
  starting transfers between devices  7.51 us (6%)
    all_to_all x2, blocking collectives, exchange(): lax.all_to_all(x, 'page', split_axis=0, concat_axis=0, axis_index_groups=...  41.9 us
    all_gather x1, blocking collectives, per_device(): rows = lax.all_gather(rows, 'page', axis_index_groups=far_groups)  37.3 us
    all_to_all x1, waiting for transfers between devices, exchange(): lax.all_to_all(x, 'page', split_axis=0, concat_axis=0, axis_index_groups=...  32 us
    pallas_call x1, Pallas kernels, per_device(): pl.pallas_call(attend_kernel, out_shape=jax.ShapeDtypeStruct((near, tall,...  8.55 us
    all_to_all x1, starting transfers between devices, exchange(): lax.all_to_all(x, 'page', split_axis=0, concat_axis=0, axis_index_groups=...  7.51 us
  transfers between devices with their start and end apart: 1, of which 1 were waited for; matrix products, arithmetic and copies ran while one was open for 0% of the time, Pallas kernels for 0%

profile of v6, /device:TPU:24, one launch (start us, length us, event | category | flops | bytes accessed | tf_op | source)
XLA Modules:
  0.0 133.7 jit_solution(13940627303213007434)
XLA Ops:
  0.0 1.6 %pack.1 = bf16[264,128]{1,0:T(8,128)(2,1)} custom-call(bf16[16,2048]{1,0:T(8,128)(2,1)} %queries_in.1, s32[8,16]{1,0:T(8,128)} %bitcast.9, s32[16,16]{1,0:T(8,128)} %bitcast.8, s32[1,16]{1,0:T(1,128)} %bitcast.10), custom_call_target="tpu_custom_call" | custom-call | tf_op jit(solution)/shard_map/pack/pallas_call | solution.py:343
  1.6 37.3 %all-gather = bf16[2112,128]{1,0:T(8,128)(2,1)S(1)} all-gather(bf16[264,128]{1,0:T(8,128)(2,1)} %pack.1), channel_id=2, replica_groups={{0,64,128,192,256,320,384,448},{4,68,132,196,260,324,388,452},{8,72,136..., dimensions={0}, use_global_device_ids=true | all-gather | bytes 608256 | tf_op jit(solution)/shard_map/all_gather | solution.py:363
  38.9 1.1 select.7
  40.0 0.0 copy-start
  40.1 0.0 copy-start.1
  40.1 22.3 %all_to_all.15.rows_ref = bf16[16,264,128]{2,1,0:T(8,128)(2,1)S(1)} all-to-all(bf16[16,264,128]{2,1,0:T(8,128)(2,1)S(1)} %get-tuple-element.7), channel_id=1, replica_groups={{0,4,8,12,16,20,24,28,32,36,40,44,48,52,56,60},{64,68,72,76,80,84,88,92..., dimensions={0} | all-to-all | bytes 2162688 | tf_op jit(solution)/shard_map/all_to_all | solution.py:339
  62.4 0.0 copy-done
  62.4 0.0 copy-done.1
  62.4 8.5 %attend.1 = bf16[16,264,128]{2,1,0:T(8,128)(2,1)S(1)} custom-call(bf16[16,264,128]{2,1,0:T(8,128)(2,1)S(1)} %all_to_all.15.rows_ref, bf16[32,64,256]{2,1,0:T(8,128)(2,1)S(1)} %copy-done, bf16[32,64,256]{2,1,0:T(8,128)(2,1)S(1)} %copy-done.1), custom_call_target="tpu_custom_call" | custom-call | tf_op jit(solution)/shard_map/attend/pallas_call | solution.py:377
  71.0 19.6 %all_to_all.16.rows_ref = bf16[16,264,128]{2,1,0:T(8,128)(2,1)S(1)} all-to-all(bf16[16,264,128]{2,1,0:T(8,128)(2,1)S(1)} %attend.1), channel_id=1, replica_groups={{0,4,8,12,16,20,24,28,32,36,40,44,48,52,56,60},{64,68,72,76,80,84,88,92..., dimensions={0} | all-to-all | bytes 2162688 | tf_op jit(solution)/shard_map/all_to_all | solution.py:339
  90.5 2.4 %merge_near.1 = bf16[8,264,128]{2,1,0:T(8,128)(2,1)} custom-call(bf16[16,264,128]{2,1,0:T(8,128)(2,1)S(1)} %all_to_all.16.rows_ref, f32[128,256]{1,0:T(8,128)S(1)} %get-tuple-element.8.sel_ref), custom_call_target="tpu_custom_call" | custom-call | tf_op jit(solution)/shard_map/merge_near/pallas_call | solution.py:396
  93.0 7.5 %all-to-all-start.2 = ((bf16[8,264,128]{2,1,0:T(8,128)(2,1)}), bf16[8,264,128]{2,1,0:T(8,128)(2,1)S(1)}, u32[]{:S(2)}, u32[]{:S(2)}) async-start(bf16[8,264,128]{2,1,0:T(8,128)(2,1)} %merge_near.1), calls=%async_computation.2 | async-start | bytes 1081344 | tf_op jit(solution)/shard_map/all_to_all | solution.py:339
  100.5 32.0 %all-to-all-done.2.rows_ref = bf16[8,264,128]{2,1,0:T(8,128)(2,1)S(1)} async-done(((bf16[8,264,128]{2,1,0:T(8,128)(2,1)}), bf16[8,264,128]{2,1,0:T(8,128)(2,1)S(1)}, u32[]{:S(2)}, u32[]{:S(2)}) %all-to-all-start.2) | async-done | bytes 540704 | tf_op jit(solution)/shard_map/all_to_all | solution.py:339
  132.5 1.3 merge_far.1
  (2 shorter events, 0.0 us)
Async XLA Ops:
  40.0 22.4 %copy-start = (bf16[32,64,256]{2,1,0:T(8,128)(2,1)S(1)}, bf16[32,64,256]{2,1,0:T(8,128)(2,1)}, u32[]{:S(2)}) copy-start(bf16[32,64,256]{2,1,0:T(8,128)(2,1)} %keys_ref.1) | copy-start | bytes 3145732
  40.1 22.4 %copy-start.1 = (bf16[32,64,256]{2,1,0:T(8,128)(2,1)S(1)}, bf16[32,64,256]{2,1,0:T(8,128)(2,1)}, u32[]{:S(2)}) copy-start(bf16[32,64,256]{2,1,0:T(8,128)(2,1)} %values_ref.1) | copy-start | bytes 3145732
  93.0 39.5 %all-to-all-start.2 = ((bf16[8,264,128]{2,1,0:T(8,128)(2,1)}), bf16[8,264,128]{2,1,0:T(8,128)(2,1)S(1)}, u32[]{:S(2)}, u32[]{:S(2)}) async-start(bf16[8,264,128]{2,1,0:T(8,128)(2,1)} %merge_near.1), calls=%async_computation.2 | async-start | bytes 1081344 | tf_op jit(solution)/shard_map/all_to_all | solution.py:339

commit v7 on v6

--- a/solution.py
+++ b/solution.py
@@ -283,41 +283,50 @@
     put_carries(out_ref, jnp.concatenate(pieces(carries), axis=0))
 
 
-def merge_kernel(last, rows_ref, sel_ref, out_ref):
+def merge_kernel(last, rows_ref, *refs):
+    out_ref = refs[-1]
     heads = (rows_ref.shape[1] - EXTRA) // TILE
     cells = rows_ref.shape[0] * TILE
-    count = sel_ref.shape[0]
-    chosen = sel_ref[...] > 0.0
+    if last:
+        count = out_ref.shape[0]
+        chosen = iota((count, cells), 1) % TILE == iota((count, cells), 0)
+    else:
+        sel = refs[0][...]
+        count = sel.shape[0]
+        chosen = sel > 0.0
     carries = get_carries(rows_ref, heads)
     lane = iota((count, LANES), 1)
-    told = jnp.zeros((count, LANES), F32)
-    some = jnp.max(sel_ref[...], axis=1, keepdims=True) > 0.0
+    highs = jnp.zeros((count, LANES), F32)
+    totals = jnp.ones((count, LANES), F32)
+    ones = jnp.ones((cells, HEAD), BF16)
     for head in range(heads):
         carry = jnp.broadcast_to(carries[head : head + 1], (count, cells))
         carry = jnp.where(chosen, carry, DEAD)
         high = jnp.max(carry, axis=1, keepdims=True)
         share = jnp.exp(carry - high)
-        total = jnp.sum(share, axis=1, keepdims=True)
-        share = share * (1.0 / total)
         major = share.astype(BF16)
         values = rows_ref[:, head * TILE : (head + 1) * TILE, :].reshape(cells, HEAD)
+        values = jnp.concatenate([values, ones], axis=1)
         if last:
             minor = (share - major.astype(F32)).astype(BF16)
             both = jnp.dot(
                 jnp.concatenate([major, minor], axis=0), values, preferred_element_type=F32
             )
-            merged = both[:count] + both[count:]
+            both = both[:count] + both[count:]
+            merged = both[:, :HEAD] / both[:, HEAD:]
             out_ref[:, head * HEAD : (head + 1) * HEAD] = merged.astype(BF16)
         else:
-            merged = jnp.dot(major, values, preferred_element_type=F32)
+            both = jnp.dot(major, values, preferred_element_type=F32)
+            merged = both[:, :HEAD] / both[:, HEAD:]
             out_ref[:, head * TILE : (head + 1) * TILE, :] = merged.astype(BF16).reshape(
                 count // TILE, TILE, HEAD
             )
-            carry = jnp.where(some, high + jnp.log(total), DEAD)
-            for n, part in enumerate(pieces(carry)):
-                told = jnp.where(lane == n * heads + head, part, told)
+            highs = jnp.where(lane == head, high, highs)
+            totals = jnp.where(lane == head, both[:, HEAD:], totals)
     if not last:
-        put_carries(out_ref, told.T[: 3 * heads])
+        some = jnp.max(sel, axis=1, keepdims=True) > 0.0
+        carry = jnp.where(some, highs + jnp.log(totals), DEAD).T[:heads]
+        put_carries(out_ref, jnp.concatenate(pieces(carry), axis=0))
 
 
 def per_device(queries, cache_keys, cache_values, routes, page_table, lengths):
@@ -402,18 +411,14 @@
         name="merge_near",
     )(partial, sel)
     partial = exchange(partial, far_groups)
-    mine = (
-        jnp.arange(count, dtype=jnp.int32)[None, :] % req_dev
-        == jnp.arange(req_dev, dtype=jnp.int32)[:, None]
-    ).astype(F32)
     return pl.pallas_call(
         functools.partial(merge_kernel, True),
         out_shape=jax.ShapeDtypeStruct((req_dev, width), BF16),
-        in_specs=[vmem] * 2,
+        in_specs=[vmem],
         out_specs=vmem,
         compiler_params=params,
         name="merge_far",
-    )(partial, mine)
+    )(partial)
 
 
 def solution(mesh):

time: 135 us -> 134 us (level)
  blocking collectives: 79.2 us -> 120 us
  waiting for transfers between devices: 32 us -> 0 us
  starting transfers between devices: 7.51 us -> 0 us
  Pallas kernels: 14.9 us -> 13.4 us
    all_to_all x2 -> x3, blocking collectives: 41.9 us -> 82.6 us  [exchange(): lax.all_to_all(x, 'page', split_axis=0, concat_axis=0, axis_index_groups=...]
    all_to_all x1 -> x0, waiting for transfers between devices: 32 us -> none  [exchange(): lax.all_to_all(x, 'page', split_axis=0, concat_axis=0, axis_index_groups=...]
    all_to_all x1 -> x0, starting transfers between devices: 7.51 us -> none  [exchange(): lax.all_to_all(x, 'page', split_axis=0, concat_axis=0, axis_index_groups=...]
    pallas_call x1, Pallas kernels: 2.44 us -> 1.03 us  [per_device(): pl.pallas_call(functools.partial(merge_kernel, False), out_shape=jax.Shap...]
  transfers between devices with their start and end apart: 1 -> 0, of which waited for: 1 -> 0; matrix products, arithmetic and copies ran while one was open for 0% -> 0% of each run, Pallas kernels for 0% -> 0%
where the time goes in v7:
time: 134 us; the launch traced here: 133 us
  blocking collectives  120 us (90%)
  Pallas kernels  13.4 us (10%)
    all_to_all x3, blocking collectives, exchange(): lax.all_to_all(x, 'page', split_axis=0, concat_axis=0, axis_index_groups=...  82.6 us
    all_gather x1, blocking collectives, per_device(): rows = lax.all_gather(rows, 'page', axis_index_groups=far_groups)  37.3 us
    pallas_call x1, Pallas kernels, per_device(): pl.pallas_call(attend_kernel, out_shape=jax.ShapeDtypeStruct((near, tall,...  8.55 us

profile of v7, /device:TPU:24, one launch (start us, length us, event | category | flops | bytes accessed | tf_op | source)
XLA Modules:
  0.0 133.5 jit_solution(17737564550411030130)
XLA Ops:
  0.0 1.6 %pack.1 = bf16[264,128]{1,0:T(8,128)(2,1)} custom-call(bf16[16,2048]{1,0:T(8,128)(2,1)} %queries_in.1, s32[8,16]{1,0:T(8,128)} %bitcast.9, s32[16,16]{1,0:T(8,128)} %bitcast.8, s32[1,16]{1,0:T(1,128)} %bitcast.10), custom_call_target="tpu_custom_call" | custom-call | tf_op jit(solution)/shard_map/pack/pallas_call | solution.py:352
  1.6 37.3 %all-gather = bf16[2112,128]{1,0:T(8,128)(2,1)S(1)} all-gather(bf16[264,128]{1,0:T(8,128)(2,1)} %pack.1), channel_id=2, replica_groups={{0,64,128,192,256,320,384,448},{4,68,132,196,260,324,388,452},{8,72,136..., dimensions={0}, use_global_device_ids=true | all-gather | bytes 608256 | tf_op jit(solution)/shard_map/all_gather | solution.py:372
  38.9 1.1 select.5
  40.0 0.0 copy-start
  40.1 0.0 copy-start.1
  40.1 22.3 %all_to_all.15.rows_ref = bf16[16,264,128]{2,1,0:T(8,128)(2,1)S(1)} all-to-all(bf16[16,264,128]{2,1,0:T(8,128)(2,1)S(1)} %get-tuple-element.7), channel_id=1, replica_groups={{0,4,8,12,16,20,24,28,32,36,40,44,48,52,56,60},{64,68,72,76,80,84,88,92..., dimensions={0} | all-to-all | bytes 2162688 | tf_op jit(solution)/shard_map/all_to_all | solution.py:348
  62.4 0.0 copy-done
  62.4 0.0 copy-done.1
  62.4 8.5 %attend.1 = bf16[16,264,128]{2,1,0:T(8,128)(2,1)S(1)} custom-call(bf16[16,264,128]{2,1,0:T(8,128)(2,1)S(1)} %all_to_all.15.rows_ref, bf16[32,64,256]{2,1,0:T(8,128)(2,1)S(1)} %copy-done, bf16[32,64,256]{2,1,0:T(8,128)(2,1)S(1)} %copy-done.1), custom_call_target="tpu_custom_call" | custom-call | tf_op jit(solution)/shard_map/attend/pallas_call | solution.py:386
  70.9 19.6 %all_to_all.16.rows_ref = bf16[16,264,128]{2,1,0:T(8,128)(2,1)S(1)} all-to-all(bf16[16,264,128]{2,1,0:T(8,128)(2,1)S(1)} %attend.1), channel_id=1, replica_groups={{0,4,8,12,16,20,24,28,32,36,40,44,48,52,56,60},{64,68,72,76,80,84,88,92..., dimensions={0} | all-to-all | bytes 2162688 | tf_op jit(solution)/shard_map/all_to_all | solution.py:348
  90.5 1.0 merge_near.1
  91.6 40.7 %all_to_all.17.rows_ref = bf16[8,264,128]{2,1,0:T(8,128)(2,1)S(1)} all-to-all(bf16[8,264,128]{2,1,0:T(8,128)(2,1)S(1)} %merge_near.1), channel_id=1, replica_groups={{0,64,128,192,256,320,384,448},{4,68,132,196,260,324,388,452},{8,72,136..., dimensions={0} | all-to-all | bytes 1081344 | tf_op jit(solution)/shard_map/all_to_all | solution.py:348
  132.3 1.2 merge_far.1
Async XLA Ops:
  40.0 22.3 %copy-start = (bf16[32,64,256]{2,1,0:T(8,128)(2,1)S(1)}, bf16[32,64,256]{2,1,0:T(8,128)(2,1)}, u32[]{:S(2)}) copy-start(bf16[32,64,256]{2,1,0:T(8,128)(2,1)} %keys_ref.1) | copy-start | bytes 3145732
  40.1 22.3 %copy-start.1 = (bf16[32,64,256]{2,1,0:T(8,128)(2,1)S(1)}, bf16[32,64,256]{2,1,0:T(8,128)(2,1)}, u32[]{:S(2)}) copy-start(bf16[32,64,256]{2,1,0:T(8,128)(2,1)} %values_ref.1) | copy-start | bytes 3145732

commit v8 on v7

--- a/solution.py
+++ b/solution.py
@@ -13,7 +13,7 @@
 SLOT = 2
 TILE = 16
 EXTRA = 8
-BLOCK = 32
+BLOCK = 64
 DEAD = -1e30
 F32 = jnp.float32
 BF16 = jnp.bfloat16
@@ -211,7 +211,7 @@
         return jnp.concatenate([ref[told_smem[which, cell]] for which in (0, 1)], axis=0)
 
     def scores(i):
-        start = pl.multiple_of(i * block, block)
+        start = i * block
         for sub in range(0, block, TILE):
             query_ref[sub * heads : (sub + TILE) * heads, :] = rows_ref[
                 i * (block // TILE) + sub // TILE, : heads * TILE, :
@@ -226,7 +226,7 @@
                 ],
                 axis=0,
             )
-            at = pl.multiple_of((start + cell) * heads, heads)
+            at = (start + cell) * heads
             score_ref[pl.ds(at, heads), :] = lax.dot_general(
                 spread.astype(BF16),
                 pages(keys_ref, start + cell),
@@ -235,9 +235,9 @@
             )
 
     def softmax(i, carries):
-        start = pl.multiple_of(i * block, block)
+        start = i * block
         for cell in range(block):
-            at = pl.multiple_of((start + cell) * heads, heads)
+            at = (start + cell) * heads
             own = score_ref[pl.ds(at, heads), :] * scale
             own = jnp.where(token < told_smem[2, start + cell], own, DEAD)
             top = jnp.max(own, axis=1, keepdims=True)
@@ -249,9 +249,9 @@
         return carries
 
     def mix(i):
-        start = pl.multiple_of(i * block, block)
+        start = i * block
         for cell in range(block):
-            at = pl.multiple_of((start + cell) * heads, heads)
+            at = (start + cell) * heads
             mixed = jnp.dot(
                 prob_ref[pl.ds(at, heads), :],
                 pages(values_ref, start + cell),
@@ -267,19 +267,14 @@
                     i * (block // TILE) + sub // TILE, head * TILE : (head + 1) * TILE, :
                 ] = mixed_ref[pl.ds(sub * heads + head, TILE, stride=heads), :].astype(BF16)
 
-    def step(i, carries):
-        mix(i - 2)
-        carries = softmax(i - 1, carries)
-        scores(i)
-        return carries
-
-    scores(0)
-    carries = softmax(0, jnp.zeros((heads, cells), F32))
-    scores(1)
-    carries = lax.fori_loop(2, blocks, step, carries)
-    mix(blocks - 2)
-    carries = softmax(blocks - 1, carries)
-    mix(blocks - 1)
+    carries = jnp.zeros((heads, cells), F32)
+    for i in range(blocks + 2):
+        if i >= 2:
+            mix(i - 2)
+        if 1 <= i <= blocks:
+            carries = softmax(i - 1, carries)
+        if i < blocks:
+            scores(i)
     put_carries(out_ref, jnp.concatenate(pieces(carries), axis=0))
 
 

time: 134 us -> 133 us (level)
  no operation moved by 1% of the time
where the time goes in v8:
time: 133 us
  blocking collectives  120 us (90%)
  Pallas kernels  12.6 us (9%)
    all_to_all x3, blocking collectives, exchange(): lax.all_to_all(x, 'page', split_axis=0, concat_axis=0, axis_index_groups=...  82.6 us
    all_gather x1, blocking collectives, per_device(): rows = lax.all_gather(rows, 'page', axis_index_groups=far_groups)  37.3 us
    pallas_call x1, Pallas kernels, per_device(): pl.pallas_call(attend_kernel, out_shape=jax.ShapeDtypeStruct((near, tall,...  7.71 us

profile of v8, /device:TPU:24, one launch (start us, length us, event | category | flops | bytes accessed | tf_op | source)
XLA Modules:
  0.0 132.6 jit_solution(12276421116780944033)
XLA Ops:
  0.0 1.6 %pack.1 = bf16[264,128]{1,0:T(8,128)(2,1)} custom-call(bf16[16,2048]{1,0:T(8,128)(2,1)} %queries_in.1, s32[8,16]{1,0:T(8,128)} %bitcast.9, s32[16,16]{1,0:T(8,128)} %bitcast.8, s32[1,16]{1,0:T(1,128)} %bitcast.10), custom_call_target="tpu_custom_call" | custom-call | tf_op jit(solution)/shard_map/pack/pallas_call | solution.py:347
  1.6 37.3 %all-gather = bf16[2112,128]{1,0:T(8,128)(2,1)S(1)} all-gather(bf16[264,128]{1,0:T(8,128)(2,1)} %pack.1), channel_id=2, replica_groups={{0,64,128,192,256,320,384,448},{4,68,132,196,260,324,388,452},{8,72,136..., dimensions={0}, use_global_device_ids=true | all-gather | bytes 608256 | tf_op jit(solution)/shard_map/all_gather | solution.py:367
  38.9 1.1 select.5
  40.0 0.0 copy-start
  40.1 0.0 copy-start.1
  40.1 22.3 %all_to_all.15.rows_ref = bf16[16,264,128]{2,1,0:T(8,128)(2,1)S(1)} all-to-all(bf16[16,264,128]{2,1,0:T(8,128)(2,1)S(1)} %get-tuple-element.7), channel_id=1, replica_groups={{0,4,8,12,16,20,24,28,32,36,40,44,48,52,56,60},{64,68,72,76,80,84,88,92..., dimensions={0} | all-to-all | bytes 2162688 | tf_op jit(solution)/shard_map/all_to_all | solution.py:343
  62.4 0.0 copy-done
  62.4 0.0 copy-done.1
  62.4 7.7 %attend.1 = bf16[16,264,128]{2,1,0:T(8,128)(2,1)S(1)} custom-call(bf16[16,264,128]{2,1,0:T(8,128)(2,1)S(1)} %all_to_all.15.rows_ref, bf16[32,64,256]{2,1,0:T(8,128)(2,1)S(1)} %copy-done, bf16[32,64,256]{2,1,0:T(8,128)(2,1)S(1)} %copy-done.1), custom_call_target="tpu_custom_call" | custom-call | tf_op jit(solution)/shard_map/attend/pallas_call | solution.py:381
  70.1 19.6 %all_to_all.16.rows_ref = bf16[16,264,128]{2,1,0:T(8,128)(2,1)S(1)} all-to-all(bf16[16,264,128]{2,1,0:T(8,128)(2,1)S(1)} %attend.1), channel_id=1, replica_groups={{0,4,8,12,16,20,24,28,32,36,40,44,48,52,56,60},{64,68,72,76,80,84,88,92..., dimensions={0} | all-to-all | bytes 2162688 | tf_op jit(solution)/shard_map/all_to_all | solution.py:343
  89.7 1.0 merge_near.1
  90.7 40.7 %all_to_all.17.rows_ref = bf16[8,264,128]{2,1,0:T(8,128)(2,1)S(1)} all-to-all(bf16[8,264,128]{2,1,0:T(8,128)(2,1)S(1)} %merge_near.1), channel_id=1, replica_groups={{0,64,128,192,256,320,384,448},{4,68,132,196,260,324,388,452},{8,72,136..., dimensions={0} | all-to-all | bytes 1081344 | tf_op jit(solution)/shard_map/all_to_all | solution.py:343
  131.5 1.2 merge_far.1
Async XLA Ops:
  40.0 22.3 %copy-start = (bf16[32,64,256]{2,1,0:T(8,128)(2,1)S(1)}, bf16[32,64,256]{2,1,0:T(8,128)(2,1)}, u32[]{:S(2)}) copy-start(bf16[32,64,256]{2,1,0:T(8,128)(2,1)} %keys_ref.1) | copy-start | bytes 3145732
  40.1 22.3 %copy-start.1 = (bf16[32,64,256]{2,1,0:T(8,128)(2,1)S(1)}, bf16[32,64,256]{2,1,0:T(8,128)(2,1)}, u32[]{:S(2)}) copy-start(bf16[32,64,256]{2,1,0:T(8,128)(2,1)} %values_ref.1) | copy-start | bytes 3145732

commit v9 on v8

--- a/solution.py
+++ b/solution.py
@@ -147,7 +147,7 @@
     before = jnp.where((a // TILE == b // TILE) & (b < a), 1.0, 0.0).astype(BF16)
     rank = jnp.dot(before, named.astype(BF16), preferred_element_type=F32)
     sel = jnp.where(rank == (lane % SLOT).astype(F32), named, 0.0)
-    sel_ref[...] = sel
+    sel_ref[...] = sel.astype(BF16)
     code = jnp.sum(sel * code, axis=0, keepdims=True)
     live = jnp.floor(code * (1.0 / 1024.0))
     code = code - 1024.0 * live
@@ -286,7 +286,7 @@
         count = out_ref.shape[0]
         chosen = iota((count, cells), 1) % TILE == iota((count, cells), 0)
     else:
-        sel = refs[0][...]
+        sel = refs[0][...].astype(F32)
         count = sel.shape[0]
         chosen = sel > 0.0
     carries = get_carries(rows_ref, heads)
@@ -303,11 +303,7 @@
         values = rows_ref[:, head * TILE : (head + 1) * TILE, :].reshape(cells, HEAD)
         values = jnp.concatenate([values, ones], axis=1)
         if last:
-            minor = (share - major.astype(F32)).astype(BF16)
-            both = jnp.dot(
-                jnp.concatenate([major, minor], axis=0), values, preferred_element_type=F32
-            )
-            both = both[:count] + both[count:]
+            both = jnp.dot(major, values, preferred_element_type=F32)
             merged = both[:, :HEAD] / both[:, HEAD:]
             out_ref[:, head * HEAD : (head + 1) * HEAD] = merged.astype(BF16)
         else:
@@ -370,7 +366,7 @@
         select_kernel,
         out_shape=(
             jax.ShapeDtypeStruct((near, tall, HEAD), BF16),
-            jax.ShapeDtypeStruct((count, cells), F32),
+            jax.ShapeDtypeStruct((count, cells), BF16),
         ),
         in_specs=[pl.BlockSpec(memory_space=pltpu.SMEM), vmem],
         out_specs=(vmem, vmem),

time: 133 us -> 133 us (level)
  no operation moved by 1% of the time
where the time goes in v9:
time: 133 us
  blocking collectives  120 us (90%)
  Pallas kernels  12.6 us (9%)
    all_to_all x3, blocking collectives, exchange(): lax.all_to_all(x, 'page', split_axis=0, concat_axis=0, axis_index_groups=...  82.7 us
    all_gather x1, blocking collectives, per_device(): rows = lax.all_gather(rows, 'page', axis_index_groups=far_groups)  37.3 us
    pallas_call x1, Pallas kernels, per_device(): pl.pallas_call(attend_kernel, out_shape=jax.ShapeDtypeStruct((near, tall,...  7.71 us

profile of v9, /device:TPU:24, one launch (start us, length us, event | category | flops | bytes accessed | tf_op | source)
XLA Modules:
  0.0 132.6 jit_solution(16052835016918116318)
XLA Ops:
  0.0 1.6 %pack.1 = bf16[264,128]{1,0:T(8,128)(2,1)} custom-call(bf16[16,2048]{1,0:T(8,128)(2,1)} %queries_in.1, s32[8,16]{1,0:T(8,128)} %bitcast.9, s32[16,16]{1,0:T(8,128)} %bitcast.8, s32[1,16]{1,0:T(1,128)} %bitcast.10), custom_call_target="tpu_custom_call" | custom-call | tf_op jit(solution)/shard_map/pack/pallas_call | solution.py:343
  1.6 37.3 %all-gather = bf16[2112,128]{1,0:T(8,128)(2,1)S(1)} all-gather(bf16[264,128]{1,0:T(8,128)(2,1)} %pack.1), channel_id=2, replica_groups={{0,64,128,192,256,320,384,448},{4,68,132,196,260,324,388,452},{8,72,136..., dimensions={0}, use_global_device_ids=true | all-gather | bytes 608256 | tf_op jit(solution)/shard_map/all_gather | solution.py:363
  38.9 1.1 select.5
  40.0 0.0 copy-start
  40.1 0.0 copy-start.1
  40.1 22.3 %all_to_all.15.rows_ref = bf16[16,264,128]{2,1,0:T(8,128)(2,1)S(1)} all-to-all(bf16[16,264,128]{2,1,0:T(8,128)(2,1)S(1)} %get-tuple-element.7), channel_id=1, replica_groups={{0,4,8,12,16,20,24,28,32,36,40,44,48,52,56,60},{64,68,72,76,80,84,88,92..., dimensions={0} | all-to-all | bytes 2162688 | tf_op jit(solution)/shard_map/all_to_all | solution.py:339
  62.4 0.0 copy-done
  62.4 0.0 copy-done.1
  62.4 7.7 %attend.1 = bf16[16,264,128]{2,1,0:T(8,128)(2,1)S(1)} custom-call(bf16[16,264,128]{2,1,0:T(8,128)(2,1)S(1)} %all_to_all.15.rows_ref, bf16[32,64,256]{2,1,0:T(8,128)(2,1)S(1)} %copy-done, bf16[32,64,256]{2,1,0:T(8,128)(2,1)S(1)} %copy-done.1), custom_call_target="tpu_custom_call" | custom-call | tf_op jit(solution)/shard_map/attend/pallas_call | solution.py:377
  70.1 19.6 %all_to_all.16.rows_ref = bf16[16,264,128]{2,1,0:T(8,128)(2,1)S(1)} all-to-all(bf16[16,264,128]{2,1,0:T(8,128)(2,1)S(1)} %attend.1), channel_id=1, replica_groups={{0,4,8,12,16,20,24,28,32,36,40,44,48,52,56,60},{64,68,72,76,80,84,88,92..., dimensions={0} | all-to-all | bytes 2162688 | tf_op jit(solution)/shard_map/all_to_all | solution.py:339
  89.7 1.0 merge_near.1
  90.7 40.7 %all_to_all.17.rows_ref = bf16[8,264,128]{2,1,0:T(8,128)(2,1)S(1)} all-to-all(bf16[8,264,128]{2,1,0:T(8,128)(2,1)S(1)} %merge_near.1), channel_id=1, replica_groups={{0,64,128,192,256,320,384,448},{4,68,132,196,260,324,388,452},{8,72,136..., dimensions={0} | all-to-all | bytes 1081344 | tf_op jit(solution)/shard_map/all_to_all | solution.py:339
  131.5 1.2 merge_far.1
Async XLA Ops:
  40.0 22.4 %copy-start = (bf16[32,64,256]{2,1,0:T(8,128)(2,1)S(1)}, bf16[32,64,256]{2,1,0:T(8,128)(2,1)}, u32[]{:S(2)}) copy-start(bf16[32,64,256]{2,1,0:T(8,128)(2,1)} %keys_ref.1) | copy-start | bytes 3145732
  40.1 22.3 %copy-start.1 = (bf16[32,64,256]{2,1,0:T(8,128)(2,1)S(1)}, bf16[32,64,256]{2,1,0:T(8,128)(2,1)}, u32[]{:S(2)}) copy-start(bf16[32,64,256]{2,1,0:T(8,128)(2,1)} %values_ref.1) | copy-start | bytes 3145732
